TPU v7x, 512 devices: a whole 4x4x16 slice. The times are simulated.
512 devices in a mesh: mode: 8 (over y, core), pb: 64 (over x, z).
Axes of the slice: x: 4, y: 4, z: 16, core: 2. Of those that a mesh axis runs over, the one named last changes fastest.
Arguments:
- g_wann: bfloat16 [256, 2, 144, 1024], P('pb', None, 'mode'), may hold values from -0.25 to 0.25
- rot_k: bfloat16 [2, 32, 8], replicated, may hold values from -1 to 1
- qpoints: int32 [3, 4096], P(None, 'pb'), may hold values from 0 to 31
- rot_kq: bfloat16 [4096, 2, 32, 32], P('pb'), may hold values from -1 to 1
- win_count: int32 [512], P('pb'), may hold values from 1 to 16, as said below
- win_start: int32 [512], P('pb'), may hold values from 0 to 16, as said below
- modes_vec: bfloat16 [4096, 2, 144, 144], P('pb', None, 'mode'), may hold values from -0.5 to 0.5
- frequencies: float32 [4096, 144], P('pb', 'mode'), may hold values from 0.5 to 4
Outputs:
- coupling: bfloat16 [4096, 2, 144, 128], P('pb', None, 'mode')
Inputs may be any that keep to these rules, and one draw needn't show every extreme that they name: `win_count`: each entry belongs to 8 consecutive q points; some block has exactly 16 bands. `win_start`: some block starts at 16.
All inputs are finite; a program needn't handle non-finite values.
Results may differ from a plain program's by a relative error of at most 0.0067.
Values may be sent and summed in bfloat16 or wider, within the bound.
A program may use at most 64 MiB of HBM per device.

v0:
```python
import jax
import jax.numpy as jnp
from jax import lax
from jax.sharding import PartitionSpec as P

NBW = 16
GRID = 32
QB = 8


two_pi = 6.283185307179586


def lattice_coords(cell_index):
    along_x = cell_index % 8 - 4
    along_y = cell_index // 8 % 8 - 4
    along_z = cell_index // 64 - 4
    return (along_x, along_y, along_z)


def phase_sum(q_coords, r_index, k_flat, col_width):
    along_x, along_y, along_z = lattice_coords(r_index)
    inner_sum = (
        q_coords[0][:, None] * along_x[None, :]
        + q_coords[1][:, None] * along_y[None, :]
        + q_coords[2][:, None] * along_z[None, :]
    )
    folded = jnp.mod(inner_sum, GRID)
    angles = folded.astype(jnp.float32) * (two_pi / GRID)
    cos_part = jnp.cos(angles).astype(jnp.bfloat16)
    sin_part = jnp.sin(angles).astype(jnp.bfloat16)
    row_count = cos_part.shape[0]
    stacked = jnp.concatenate([cos_part, sin_part], axis=0)
    product = jnp.dot(stacked, k_flat, preferred_element_type=jnp.float32)
    real_part = product[:row_count, :col_width] - product[row_count:, col_width:]
    imag_part = product[:row_count, col_width:] + product[row_count:, :col_width]
    return jnp.stack([real_part, imag_part], axis=1).astype(jnp.bfloat16)


def rotate_mode(vectors, blocks):

    def contract(first_op, second_op):
        return jnp.einsum("qvc,qcx->qvx", first_op, second_op, preferred_element_type=jnp.float32)

    real_part = contract(vectors[:, 0], blocks[:, 0]) - contract(vectors[:, 1], blocks[:, 1])
    imag_part = contract(vectors[:, 0], blocks[:, 1]) + contract(vectors[:, 1], blocks[:, 0])
    return jnp.stack([real_part, imag_part], axis=1)


def shards(g_wann, rot_k, qpoints, rot_kq, win_count, win_start, modes_vec, frequencies):
    r_local = g_wann.shape[0]
    c_local = g_wann.shape[2]
    n_wann = rot_k.shape[1]
    k_bands = rot_k.shape[2]
    q_local = qpoints.shape[1]
    col_width = c_local * n_wann * k_bands
    wannier = g_wann.reshape(r_local, 2, c_local, n_wann, n_wann)

    def rotate_k(first_op, second_op):
        return jnp.einsum("rcij,jb->rcib", first_op, second_op, preferred_element_type=jnp.float32)

    k_real = rotate_k(wannier[:, 0], rot_k[0]) - rotate_k(wannier[:, 1], rot_k[1])
    k_imag = rotate_k(wannier[:, 0], rot_k[1]) + rotate_k(wannier[:, 1], rot_k[0])
    k_side = jnp.stack([k_real, k_imag], axis=1).astype(jnp.bfloat16).reshape(r_local, 2, col_width)
    all_k = lax.all_gather(k_side, "pb", axis=0, tiled=True)
    total_r = all_k.shape[0]
    r_index = jnp.arange(total_r, dtype=jnp.int32)
    q_sum = phase_sum(qpoints, r_index, all_k.reshape(total_r, 2 * col_width), col_width)
    q_grid = q_sum.reshape(q_local, 2, c_local, n_wann, k_bands)
    counts_q = jnp.repeat(win_count, QB, total_repeat_length=q_local)
    starts_q = jnp.repeat(win_start, QB, total_repeat_length=q_local)
    column = jnp.arange(n_wann, dtype=jnp.int32)[None, :, None]
    slot_index = jnp.arange(NBW, dtype=jnp.int32)[None, None, :]
    picker = (
        (column == starts_q[:, None, None] + slot_index) & (slot_index < counts_q[:, None, None])
    ).astype(jnp.bfloat16)
    window = jnp.einsum(
        "qpij,qjm->qpim", rot_kq, picker, preferred_element_type=jnp.float32
    ).astype(jnp.bfloat16)

    def rotate_band(first_op, second_op):
        return jnp.einsum("qim,qcib->qcmb", first_op, second_op, preferred_element_type=jnp.float32)

    band_real = rotate_band(window[:, 0], q_grid[:, 0]) + rotate_band(window[:, 1], q_grid[:, 1])
    band_imag = rotate_band(window[:, 0], q_grid[:, 1]) - rotate_band(window[:, 1], q_grid[:, 0])
    band_blocks = (
        jnp.stack([band_real, band_imag], axis=1)
        .astype(jnp.bfloat16)
        .reshape(q_local, 2, c_local, NBW * k_bands)
    )
    sub_band, sub_vectors = (
        lax.all_to_all(band_blocks, "mode", split_axis=0, concat_axis=2, tiled=True),
        lax.all_to_all(modes_vec, "mode", split_axis=0, concat_axis=2, tiled=True),
    )
    sub_freq = lax.all_to_all(
        frequencies.reshape(q_local, 1, c_local), "mode", split_axis=0, concat_axis=2, tiled=True
    )
    share_scale = 1.0 / jnp.sqrt(2.0 * sub_freq)
    finished = (rotate_mode(sub_vectors, sub_band) * share_scale[:, :, :, None]).astype(
        jnp.bfloat16
    )
    return lax.all_to_all(finished, "mode", split_axis=2, concat_axis=0, tiled=True)


def solution(mesh):
    placed = (
        P("pb", None, "mode", None),
        P(),
        P(None, "pb"),
        P("pb", None, None, None),
        P("pb"),
        P("pb"),
        P("pb", None, "mode", None),
        P("pb", "mode"),
    )
    return jax.shard_map(
        shards, mesh=mesh, in_specs=placed, out_specs=P("pb", None, "mode", None), check_vma=False
    )
```

profile of v0, /device:TPU:1, one launch (start us, length us, event | category | flops | bytes accessed | tf_op | source)
XLA Modules:
  0.0 288.7 jit_solution(13851405062908539349)
XLA Ops:
  6.5 2.1 reshape.190
  8.6 1.5 fusion.16
  10.1 0.9 fusion.15
  11.0 0.9 fusion.8
  11.9 0.3 copy.100
  12.2 0.7 stack.30
  12.9 0.0 copy-start.8
  13.0 0.9 fusion.9
  13.9 0.3 copy.101
  14.2 0.7 stack.31
  14.8 0.1 pad_maximum_fusion.1
  14.9 0.7 copy.102
  15.6 0.0 all-gather.2.cloned.1.call-update
  15.6 0.1 copy.122
  15.7 0.5 broadcast.290
  16.2 0.7 reduce.3
  16.9 0.7 reshape.244
  17.6 10.1 %all-to-all-start.2 = ((f32[8,1,144]{2,1,0:T(1,128)}), f32[8,1,144]{2,1,0:T(1,128)S(1)}, u32[]{:S(2)}, u32[]{:S(2)}) async-start(f32[8,1,144]{2,1,0:T(1,128)} %reshape.244), calls=%async_computation.2 | async-start | bytes 16384 | tf_op jit(solution)/shard_map/all_to_all | solution.py:95
  27.7 1.6 copy.105
  29.3 0.7 fusion.46
  30.0 0.7 fusion.45
  30.8 5.1 %select_select_fusion.1 = s32[64]{0:T(128)S(1)} fusion(pred[64]{0:T(512)(128)(4,1)S(1)} %copy-done.8, pred[64]{0:T(512)(128)(4,1)S(1)} %copy-done.9, pred[64]{0:T(512)(128)(4,1)S(1)} %copy-done.10, pred[64]{0:T(512)(128)(4,1)S(1)} %copy-done.11, pred[64]{0:T(512)(128)(4,1)S(1)} %copy-done.12, pred[64]{0:T(512)(128)(4,1)S(1)} %copy-done.13, ...), kind=kLoop, calls=%fused_computation.85 | loop fusion | flops 448 | bytes 736 | tf_op jit(solution)/shard_map/jit(_take)/gather | solution.py:71
  35.8 5.0 %select_select_fusion = s32[64]{0:T(128)S(1)} fusion(pred[64]{0:T(512)(128)(4,1)S(1)} %copy-done.8, pred[64]{0:T(512)(128)(4,1)S(1)} %copy-done.9, pred[64]{0:T(512)(128)(4,1)S(1)} %copy-done.10, pred[64]{0:T(512)(128)(4,1)S(1)} %copy-done.11, pred[64]{0:T(512)(128)(4,1)S(1)} %copy-done.12, pred[64]{0:T(512)(128)(4,1)S(1)} %copy-done.13, ...), kind=kLoop, calls=%fused_computation.84 | loop fusion | flops 448 | bytes 736 | tf_op jit(solution)/shard_map/jit(_take)/gather | solution.py:70
  40.8 0.1 iota_compare_fusion.1
  40.9 0.1 iota_add_fusion
  41.0 0.4 cosine_convert_fusion
  41.3 2.3 fusion.4
  43.6 117.1 %all-gather.2.cloned.1.call-done = bf16[256,2,4608]{2,1,0:T(2,128)(2,1)} async-done(((bf16[4,2,4608]{2,1,0:T(2,128)(2,1)}), bf16[256,2,4608]{2,1,0:T(2,128)(2,1)}) %all-gather.2.cloned.1.call-update) | async-done | bytes 4718608 | tf_op jit(solution)/shard_map/all_gather | solution.py:65
  160.7 12.3 %copy.103 = bf16[256,2,4608]{0,2,1:T(8,128)(2,1)} copy(bf16[256,2,4608]{2,1,0:T(2,128)(2,1)} %all-gather.2.cloned.1.call-done) | data formatting | bytes 9437184 | tf_op jit(solution)/shard_map/all_gather | solution.py:65
  173.1 4.0 %fusion.24 = f32[128,9216]{1,0:T(8,128)S(1)} fusion(bf16[256,9216]{0,1:T(8,128)(2,1)} %bitcast.146, bf16[64,256]{1,0:T(8,128)(2,1)S(1)} %get-tuple-element.33, bf16[64,256]{1,0:T(8,128)(2,1)S(1)} %get-tuple-element.32), kind=kOutput, calls=%fused_computation.50 | convolution fusion | flops 604110848 | bytes 9502720 | tf_op jit(solution)/shard_map/dot_general | solution.py:34
  177.1 1.0 fusion.6
  178.1 1.4 copy.104
  179.5 6.7 %copy.106 = bf16[64,18,32,8]{2,1,3,0:T(8,128)(2,1)S(1)} copy(bf16[64,18,32,8]{0,3,2,1:T(8,128)(2,1)} %bitcast.149) | data formatting | bytes 1179648 | tf_op jit(solution)/shard_map/squeeze | solution.py:84
  186.2 2.3 copy.107
  188.5 7.3 %copy.108 = bf16[64,18,32,8]{2,1,3,0:T(8,128)(2,1)} copy(bf16[64,18,32,8]{0,3,2,1:T(8,128)(2,1)} %bitcast.150) | data formatting | bytes 1179648 | tf_op jit(solution)/shard_map/squeeze | solution.py:84
  195.8 6.4 %fusion.20 = f32[64,18,8,16]{1,3,2,0:T(8,128)S(1)} fusion(bf16[64,18,32,8]{2,1,3,0:T(8,128)(2,1)S(1)} %copy.106, bf16[64,2,32,16]{2,3,1,0:T(8,128)(2,1)} %fusion.4), kind=kOutput, calls=%fused_computation.42 | convolution fusion | flops 9437184 | bytes 1441792 | tf_op jit(solution)/shard_map/qim,qcib->qcmb/dot_general | solution.py:82
  202.1 6.7 %fusion = bf16[64,18,16,8]{1,2,3,0:T(8,128)(2,1)} fusion(f32[64,18,8,16]{1,3,2,0:T(8,128)S(1)} %fusion.20, bf16[64,18,32,8]{2,1,3,0:T(8,128)(2,1)S(1)} %copy-done, bf16[64,2,32,16]{2,3,1,0:T(8,128)(2,1)S(1)} %copy-done.1), kind=kOutput, calls=%fused_computation.2 | convolution fusion | flops 9732096 | bytes 7897088 | tf_op jit(solution)/shard_map/qim,qcib->qcmb/dot_general | solution.py:82
  208.8 7.2 %fusion.19 = f32[64,18,8,16]{1,3,2,0:T(8,128)} fusion(bf16[64,18,32,8]{2,1,3,0:T(8,128)(2,1)S(1)} %copy-done, bf16[64,2,32,16]{2,3,1,0:T(8,128)(2,1)S(1)} %copy-done.1), kind=kOutput, calls=%fused_computation.41 | convolution fusion | flops 9437184 | bytes 3997696 | tf_op jit(solution)/shard_map/qim,qcib->qcmb/dot_general | solution.py:82
  216.1 4.8 %copy.109 = bf16[64,18,16,8]{0,3,2,1:T(8,128)(2,1)} copy(bf16[64,18,16,8]{1,2,3,0:T(8,128)(2,1)} %fusion) | data formatting | bytes 589824 | tf_op jit(solution)/shard_map/add | solution.py:84
  220.8 12.8 %all-to-all-start.1 = ((bf16[64,2,18,144]{3,1,2,0:T(2,128)(2,1)}), bf16[64,2,18,144]{3,1,2,0:T(2,128)(2,1)}, u32[]{:S(2)}, u32[]{:S(2)}) async-start(bf16[64,2,18,144]{3,1,2,0:T(2,128)(2,1)} %param.20), calls=%async_computation.1 | async-start | bytes 2359296 | tf_op jit(solution)/shard_map/all_to_all | solution.py:93
  233.6 8.9 %fusion.1 = bf16[64,18,16,8]{1,2,3,0:T(8,128)(2,1)} fusion(f32[64,18,8,16]{1,3,2,0:T(8,128)} %fusion.19, bf16[64,18,32,8]{2,1,3,0:T(8,128)(2,1)S(1)} %copy.106, bf16[64,2,32,16]{2,3,1,0:T(8,128)(2,1)} %fusion.4), kind=kOutput, calls=%fused_computation.3 | convolution fusion | flops 9732096 | bytes 5341184 | tf_op jit(solution)/shard_map/qim,qcib->qcmb/dot_general | solution.py:82
  242.6 4.2 %copy.112 = bf16[64,18,16,8]{0,3,2,1:T(8,128)(2,1)S(1)} copy(bf16[64,18,16,8]{1,2,3,0:T(8,128)(2,1)} %fusion.1) | data formatting | bytes 589824 | tf_op jit(solution)/shard_map/sub | solution.py:85
  246.8 0.3 pad_maximum_fusion
  247.1 1.8 copy.113
  248.8 1.4 all-to-all-done.1
  250.2 4.3 %all-to-all-start = ((bf16[64,2,18,128]{3,1,2,0:T(2,128)(2,1)}), bf16[64,2,18,128]{3,1,2,0:T(2,128)(2,1)S(1)}, u32[]{:S(2)}, u32[]{:S(2)}) async-start(bf16[64,2,18,128]{3,1,2,0:T(2,128)(2,1)} %copy.113), calls=%async_computation | async-start | bytes 1179648 | tf_op jit(solution)/shard_map/all_to_all | solution.py:92
  254.5 0.6 reduce.4
  255.2 0.1 reshape.245
  255.3 0.1 sqrt.12
  255.4 1.5 copy.156
  256.9 0.1 copy.118
  257.0 0.1 fusion.43
  257.1 7.7 %all-to-all-done = bf16[64,2,18,128]{3,1,2,0:T(2,128)(2,1)S(1)} async-done(((bf16[64,2,18,128]{3,1,2,0:T(2,128)(2,1)}), bf16[64,2,18,128]{3,1,2,0:T(2,128)(2,1)S(1)}, u32[]{:S(2)}, u32[]{:S(2)}) %all-to-all-start) | async-done | bytes 589856 | tf_op jit(solution)/shard_map/all_to_all | solution.py:92
  264.7 0.1 copy.158
  264.9 0.1 copy.115
  265.0 0.3 fusion.13
  265.3 0.3 fusion.14
  265.7 0.3 fusion.2
  266.0 0.3 fusion.3
  266.3 0.2 fusion.7
  266.5 0.2 copy.125
  266.7 13.6 %all_to_all.63 = bf16[8,2,144,128]{3,0,1,2:T(8,128)(2,1)S(1)} all-to-all(bf16[8,2,144,128]{3,0,1,2:T(8,128)(2,1)S(1)} %copy.125), channel_id=1, replica_groups=mesh['mode'=8,'pb'=64] {'mode'}, dimensions={2} | all-to-all | bytes 1179648 | tf_op jit(solution)/shard_map/all_to_all | solution.py:102
  280.3 0.2 copy.157
  280.5 1.4 copy.128
  (39 shorter events, 0.2 us)
Async XLA Ops:
  6.5 3.6 %copy-start.6 = (bf16[2,32,8]{1,2,0:T(8,128)(2,1)S(1)}, bf16[2,32,8]{1,2,0:T(8,128)(2,1)}, u32[]{:S(2)}) copy-start(bf16[2,32,8]{1,2,0:T(8,128)(2,1)} %param.15) | copy-start | bytes 3076
  6.5 154.2 %all-gather.2.cloned.1.call-start = ((), (), s32[]{:S(2)}) async-start(), calls=%async_computation.4 | async-start | bytes 4792320 | tf_op jit(solution)/shard_map/all_gather | solution.py:65
  11.9 3.7 %copy-start.7 = (f32[64,18]{0,1:T(8,128)S(1)}, f32[64,18]{0,1:T(8,128)}, u32[]{:S(2)}) copy-start(f32[64,18]{0,1:T(8,128)} %param.21) | copy-start | bytes 13828
  11.9 15.8 %copy-start.3 = (bf16[64,2,32,32]{0,3,2,1:T(8,128)(2,1)S(1)}, bf16[64,2,32,32]{0,3,2,1:T(8,128)(2,1)}, u32[]{:S(2)}) copy-start(bf16[64,2,32,32]{0,3,2,1:T(8,128)(2,1)} %param.17) | copy-start | bytes 786436
  12.9 16.4 %copy-start.4 = (s32[8]{0:T(128)S(1)}, s32[8]{0:T(128)}, u32[]{:S(2)}) copy-start(s32[8]{0:T(128)} %param.19) | copy-start | bytes 100
  12.9 17.1 %copy-start.5 = (s32[8]{0:T(128)S(1)}, s32[8]{0:T(128)}, u32[]{:S(2)}) copy-start(s32[8]{0:T(128)} %param.18) | copy-start | bytes 100
  12.9 17.8 %copy-start.15 = (s32[3,64]{1,0:T(4,128)S(1)}, s32[3,64]{1,0:T(4,128)}, u32[]{:S(2)}) copy-start(s32[3,64]{1,0:T(4,128)} %param.16) | copy-start | bytes 2308
  12.9 17.8 %copy-start.8 = (pred[64]{0:T(512)(128)(4,1)S(1)}, pred[64]{0:T(512)(128)(4,1)}, u32[]{:S(2)}) copy-start(pred[64]{0:T(512)(128)(4,1)} %constant.199) | copy-start | bytes 196
  12.9 17.8 %copy-start.9 = (pred[64]{0:T(512)(128)(4,1)S(1)}, pred[64]{0:T(512)(128)(4,1)}, u32[]{:S(2)}) copy-start(pred[64]{0:T(512)(128)(4,1)} %constant.200) | copy-start | bytes 196
  12.9 17.8 %copy-start.10 = (pred[64]{0:T(512)(128)(4,1)S(1)}, pred[64]{0:T(512)(128)(4,1)}, u32[]{:S(2)}) copy-start(pred[64]{0:T(512)(128)(4,1)} %constant.201) | copy-start | bytes 196
  13.0 17.8 %copy-start.11 = (pred[64]{0:T(512)(128)(4,1)S(1)}, pred[64]{0:T(512)(128)(4,1)}, u32[]{:S(2)}) copy-start(pred[64]{0:T(512)(128)(4,1)} %constant.202) | copy-start | bytes 196
  13.0 17.8 %copy-start.12 = (pred[64]{0:T(512)(128)(4,1)S(1)}, pred[64]{0:T(512)(128)(4,1)}, u32[]{:S(2)}) copy-start(pred[64]{0:T(512)(128)(4,1)} %constant.203) | copy-start | bytes 196
  13.0 17.8 %copy-start.13 = (pred[64]{0:T(512)(128)(4,1)S(1)}, pred[64]{0:T(512)(128)(4,1)}, u32[]{:S(2)}) copy-start(pred[64]{0:T(512)(128)(4,1)} %constant.204) | copy-start | bytes 196
  13.0 17.8 %copy-start.14 = (pred[64]{0:T(512)(128)(4,1)S(1)}, pred[64]{0:T(512)(128)(4,1)}, u32[]{:S(2)}) copy-start(pred[64]{0:T(512)(128)(4,1)} %constant.205) | copy-start | bytes 196
  17.6 203.2 %all-to-all-start.2 = ((f32[8,1,144]{2,1,0:T(1,128)}), f32[8,1,144]{2,1,0:T(1,128)S(1)}, u32[]{:S(2)}, u32[]{:S(2)}) async-start(f32[8,1,144]{2,1,0:T(1,128)} %reshape.244), calls=%async_computation.2 | async-start | bytes 16384 | tf_op jit(solution)/shard_map/all_to_all | solution.py:95
  195.8 6.4 %copy-start = (bf16[64,18,32,8]{2,1,3,0:T(8,128)(2,1)S(1)}, bf16[64,18,32,8]{2,1,3,0:T(8,128)(2,1)}, u32[]{:S(2)}) copy-start(bf16[64,18,32,8]{2,1,3,0:T(8,128)(2,1)} %copy.108) | copy-start | bytes 1769476
  195.8 6.4 %copy-start.1 = (bf16[64,2,32,16]{2,3,1,0:T(8,128)(2,1)S(1)}, bf16[64,2,32,16]{2,3,1,0:T(8,128)(2,1)}, u32[]{:S(2)}) copy-start(bf16[64,2,32,16]{2,3,1,0:T(8,128)(2,1)} %fusion.4) | copy-start | bytes 393220
  220.8 29.4 %all-to-all-start.1 = ((bf16[64,2,18,144]{3,1,2,0:T(2,128)(2,1)}), bf16[64,2,18,144]{3,1,2,0:T(2,128)(2,1)}, u32[]{:S(2)}, u32[]{:S(2)}) async-start(bf16[64,2,18,144]{3,1,2,0:T(2,128)(2,1)} %param.20), calls=%async_computation.1 | async-start | bytes 2359296 | tf_op jit(solution)/shard_map/all_to_all | solution.py:93
  242.6 4.2 %copy-start.2 = (bf16[64,18,16,8]{0,3,2,1:T(8,128)(2,1)S(1)}, bf16[64,18,16,8]{0,3,2,1:T(8,128)(2,1)}, u32[]{:S(2)}) copy-start(bf16[64,18,16,8]{0,3,2,1:T(8,128)(2,1)} %copy.109) | copy-start | bytes 884740
  250.2 14.5 %all-to-all-start = ((bf16[64,2,18,128]{3,1,2,0:T(2,128)(2,1)}), bf16[64,2,18,128]{3,1,2,0:T(2,128)(2,1)S(1)}, u32[]{:S(2)}, u32[]{:S(2)}) async-start(bf16[64,2,18,128]{3,1,2,0:T(2,128)(2,1)} %copy.113), calls=%async_computation | async-start | bytes 1179648 | tf_op jit(solution)/shard_map/all_to_all | solution.py:92
Sparse Core Ops, SparseCore 0:
  15.7 144.9 all-gather.1
where the time goes:
time: 290 us; the launch traced here: 289 us
  waiting for transfers between devices  126 us (43%)
  local copies, waits for them, and re-layouts  53.6 us (18%)
  matrix products  40.9 us (14%)
  starting transfers between devices  27.1 us (9%)
  between operations  13.8 us (5%)
  blocking collectives  13.6 us (5%)
  other arithmetic  13.5 us (5%)
    all_gather x1, waiting for transfers between devices, shards(): all_k = lax.all_gather(k_side, 'pb', axis=0, tiled=True)  117 us
    dot_general x4, matrix products, rotate_band(): jnp.einsum('qim,qcib->qcmb', first_op, second_op, preferred_element_type=...  29.2 us
    all_to_all x1, blocking collectives, shards(): lax.all_to_all(finished, 'mode', split_axis=2, concat_axis=0, tiled=True)  13.6 us
    all_to_all x1, starting transfers between devices, shards(): lax.all_to_all(modes_vec, 'mode', split_axis=0, concat_axis=2, tiled=True)  12.8 us
    all_gather x1, local copies, waits for them, and re-layouts, shards(): all_k = lax.all_gather(k_side, 'pb', axis=0, tiled=True)  12.3 us
    all_to_all x1, starting transfers between devices, shards(): lax.all_to_all(frequencies.reshape(q_local, 1, c_local), 'mode', split_ax...  10.1 us
    all_to_all x1, waiting for transfers between devices, shards(): lax.all_to_all(band_blocks, 'mode', split_axis=0, concat_axis=2, tiled=True)  7.68 us
    squeeze x1, local copies, waits for them, and re-layouts, shards(): q_grid[:, 1]  7.29 us
  transfers between devices with their start and end apart: 4, of which 3 were waited for; matrix products, arithmetic and copies ran while one was open for 33% of the time, Pallas kernels for 0%

commit v1 on v0

v1 whole, which is shorter than its diff:
```python
import functools
import jax
import jax.numpy as jnp
import numpy as np
from jax import lax
from jax.experimental import pallas as pl
from jax.experimental.pallas import tpu as pltpu
from jax.sharding import PartitionSpec as P

NX = 4
NM = 8
TWO_PI = 6.283185307179586
BF = jnp.bfloat16
F32 = jnp.float32


def dot(a, b):
    return jnp.dot(a, b, preferred_element_type=F32)


def constants(nz):
    rows = np.arange(nz * 16)
    z, x, r4 = rows // 16, rows // 4 % 4, rows % 4
    r = (x * nz + z) * 4 + r4
    lattice = np.zeros((128, nz * 16), np.float32)
    lattice[0] = r % 8 - 4
    lattice[1] = r // 8 % 8 - 4
    lattice[2] = r // 64 - 4

    row, lane = np.arange(256)[:, None], np.arange(128)[None, :]
    same = row // 32 == lane // 16
    shift = np.where(same, row % 32 - lane % 16, -1000).astype(np.int32)

    spread = np.zeros((2, 4, 2, 16, 4, 2, 2, 2, 2, 16, 2), np.float32)
    for par in range(2):
        for q4 in range(4):
            for m in range(16):
                for b in range(2):
                    spread[par, q4, 0, m, q4, 0, b, par, 0, m, b] = 1
                    spread[par, q4, 1, m, q4, 1, b, par, 0, m, b] = 1
                    spread[par, q4, 1, m, q4, 0, b, par, 1, m, b] = -1
                    spread[par, q4, 0, m, q4, 1, b, par, 1, m, b] = 1
    spread = spread.reshape(2, 128, 2048)

    pick = np.zeros((384, 1536), np.float32)
    for ri in range(2):
        for c in range(144):
            source = ri * 128 + c if c < 128 else 256 + ri * 16 + c - 128
            for q4 in range(4):
                pick[source, ri * 640 + c // 18 * 80 + q4 * 20 + c % 18] = 1
    pick[288:291, 1280:] = 1
    mask = np.zeros((2, 2, 4, 18, 8, 4, 20), np.float32)
    for par in range(2):
        for q4 in range(4):
            mask[par, par, q4, :, :, q4, :] = 1
    mask = mask.reshape(2, 144, 640)

    order = np.zeros((4, 2, 2, 16, 2, 2, 2, 2, 16, 8), np.float32)
    for xx in range(4):
        for par in range(2):
            for m in range(16):
                for b in range(2):
                    order[xx, par, 0, m, b, par, 0, 0, m, xx * 2 + b] = 1
                    order[xx, par, 1, m, b, par, 0, 1, m, xx * 2 + b] = 1
                    order[xx, par, 1, m, b, par, 1, 0, m, xx * 2 + b] = -1
                    order[xx, par, 0, m, b, par, 1, 1, m, xx * 2 + b] = 1
    order = order.reshape(512, 1024)
    half = lambda a: jnp.asarray(a, BF)
    return half(lattice), jnp.asarray(shift), half(spread), half(pick), half(mask), half(order)


def kernel(
    nz, ws_ref, wc_ref, g_ref, base_ref, qm_ref, rotq_ref, modes_ref,
    lattice_ref, shift_ref, spread_ref, pick_ref, mask_ref, order_ref, o_ref,
    gl, kw, kf, ksend, krecv, kx, ka, kbuf, ph, win, wq, qbuf, bsend, brecv, mrecv, lhs, scale, rhs, osend,
    ks_sem, kr_sem, ps_sem, pr_sem, ns_sem, nr_sem, ms_sem, mr_sem, zs_sem, zr_sem, bs_sem, br_sem, os_sem, or_sem,
):
    me = lax.axis_index("mode")
    pb = lax.axis_index("pb")
    x, z = pb // nz, pb % nz
    nr = nz * 16

    def at(xx, mm):
        return {"mode": mm, "pb": xx * nz + z}

    def remote(src, dst, ssem, rsem, where):
        return pltpu.make_async_remote_copy(
            src_ref=src, dst_ref=dst, send_sem=ssem, recv_sem=rsem,
            device_id=where, device_id_type=pl.DeviceIdType.MESH,
        )

    right = {"mode": me, "pb": x * nz + (z + 1) % nz}
    left = {"mode": me, "pb": x * nz + (z + nz - 1) % nz}

    barrier = pltpu.get_barrier_semaphore()

    @pl.loop(1, 32)
    def _(d):
        pl.semaphore_signal(
            barrier, inc=1, device_id=at((x + d // 8) % 4, (me + d) % 8), device_id_type=pl.DeviceIdType.MESH
        )

    if nz > 1:
        pl.semaphore_signal(barrier, inc=1, device_id=left, device_id_type=pl.DeviceIdType.MESH)
        pl.semaphore_signal(barrier, inc=1, device_id=right, device_id_type=pl.DeviceIdType.MESH)

    lane_i = lax.broadcasted_iota(jnp.int32, (32, 512), 1) % 32
    for ri in range(2):
        part = base_ref[ri * 32:(ri + 1) * 32, :]

        @pl.loop(0, 32)
        def _(i):
            kw[pl.ds(pl.multiple_of(ri * 1024 + i * 32, 32), 32), :] = jnp.where(lane_i == i, part, 0.0).astype(BF)

    for r in range(4):
        for ri in range(2):
            gl[r * 32:r * 32 + 18, ri * 1024:(ri + 1) * 1024] = g_ref[r, ri]
    turned = dot(gl[...], kw[...])
    kf[...] = jnp.zeros_like(kf)
    for xx in range(4):
        for r in range(4):
            kf[xx, pl.ds(r, 18, stride=4), :] = turned[r * 32:r * 32 + 18, xx * 128:(xx + 1) * 128]
    ksend[...] = kf[...].astype(BF)

    pl.semaphore_wait(barrier, 31 + (2 if nz > 1 else 0))

    for d in range(1, 4):
        xx = (x + d) % 4
        remote(ksend.at[xx], krecv.at[x], ks_sem.at[xx], kr_sem.at[x], at(xx, me)).start()
    krecv[x] = ksend[x]

    inner = dot(qm_ref[...], lattice_ref[...]).astype(jnp.int32) & 31
    angle = inner.astype(F32) * (TWO_PI / 32)
    ph[x, 0:64, :] = jnp.cos(angle).astype(BF)
    ph[x, 64:128, :] = jnp.sin(angle).astype(BF)
    for d in range(1, 4):
        xx = (x + d) % 4
        remote(ph.at[x], ph.at[x], ps_sem.at[xx], pr_sem.at[x], at(xx, me)).start()

    for d in range(1, 8):
        mm = (me + d) % 8
        remote(modes_ref.at[mm], mrecv.at[me], ms_sem.at[mm], mr_sem.at[me], at(x, mm)).start()
    mrecv[me] = modes_ref[me]

    lane_m = lax.broadcasted_iota(jnp.int32, (256, 128), 1) % 16
    for t in range(8):
        chosen = jnp.where((shift_ref[...] == ws_ref[t]) & (lane_m < wc_ref[t]), 1.0, 0.0).astype(BF)
        cut = dot(rotq_ref[t], chosen).astype(BF)
        win[x, 0, t * 32:(t + 1) * 32, :] = cut[0:32]
        win[x, 1, t * 32:(t + 1) * 32, :] = cut[32:64]
    for d in range(1, 4):
        xx = (x + d) % 4
        remote(win.at[x], win.at[x], ns_sem.at[xx], nr_sem.at[x], at(xx, me)).start()

    for d in range(1, 4):
        xx = (x + d) % 4
        remote(ksend.at[xx], krecv.at[xx], ks_sem.at[xx], kr_sem.at[xx], at(xx, me)).wait_recv()
    kx[...] = krecv[...].astype(F32)
    for xx in range(4):
        for r in range(4):
            ka[pl.ds(xx * 4 + r, 18, stride=16), :] = kx[xx, pl.ds(r, 18, stride=4), :]
    kbuf[z] = ka[...].astype(BF)

    def hop(way, step, part):
        shard = (z + (nz - step if way == 0 else step)) % nz
        piece = kbuf.at[shard, pl.ds(part * 144, 144)]
        return remote(piece, piece, zs_sem.at[way, step, part], zr_sem.at[way, step, part], right if way == 0 else left)

    hops = (nz // 2, nz - 1 - nz // 2)

    def weights(xx):
        for par in range(2):
            for q4 in range(4):
                spreaded = dot(win[xx, par], spread_ref[par, :, q4 * 512:(q4 + 1) * 512]).astype(BF)
                for g in range(4):
                    rows = spreaded[:, g * 128:(g + 1) * 128].reshape(8, 32, 128)
                    start = par * 128 + g * 32
                    wq[pl.ds(xx * 8, 8), q4, start:start + 32, :] = rows

    def vectors(mm):
        spreaded = dot(mrecv[mm], pick_ref[...])
        scale[mm] = spreaded[:, 1280:]
        both = spreaded[:, :1280].astype(BF)
        for par in range(2):
            for ri in range(2):
                start = (par * 2 + ri) * 640
                lhs[mm, :, start:start + 640] = both[:, ri * 640:(ri + 1) * 640] * mask_ref[par]

    def wait_window(xx):
        remote(win.at[xx], win.at[xx], ns_sem.at[xx], nr_sem.at[xx], at(xx, me)).wait_recv()

    def wait_vectors(mm):
        remote(modes_ref.at[mm], mrecv.at[mm], ms_sem.at[mm], mr_sem.at[mm], at(x, mm)).wait_recv()

    for step in range(8):
        for part in range(2):
            for way in range(2):
                if step < hops[way]:
                    if step > 0:
                        hop(way, step - 1, part).wait_recv()
                    hop(way, step, part).start()
        if step < 4:
            xx = (x + step) % 4
            if step > 0:
                wait_window(xx)
            weights(xx)
        mm = (me + step) % 8
        if step > 0:
            wait_vectors(mm)
        vectors(mm)
    for way in range(2):
        if hops[way]:
            for part in range(2):
                hop(way, hops[way] - 1, part).wait_recv()

    for d in range(1, 4):
        xx = (x + d) % 4
        remote(ph.at[xx], ph.at[xx], ps_sem.at[xx], pr_sem.at[xx], at(xx, me)).wait_recv()
    qbuf[...] = jnp.zeros_like(qbuf)
    turn = lax.broadcasted_iota(jnp.int32, (64, 128), 1) < 64

    @pl.loop(0, 9)
    def _(cp):
        pair = [
            kbuf[:, pl.ds(pl.multiple_of((cp * 2 + p) * 16, 16), 16), :].reshape(nr, 128) for p in range(2)
        ]
        both = dot(ph[...].reshape(512, nr), jnp.concatenate(pair, axis=1))
        for p in range(2):
            for xx in range(4):
                along = both[xx * 128:xx * 128 + 64, p * 128:(p + 1) * 128]
                across = pltpu.roll(both[xx * 128 + 64:xx * 128 + 128, p * 128:(p + 1) * 128], 64, 1)
                total = along + jnp.where(turn, -across, across)
                for par in range(2):
                    qbuf[par, pl.ds(xx * 640 + cp * 2 + p, 32, stride=20), :] = total[par * 32:(par + 1) * 32]

    row = lax.broadcasted_iota(jnp.int32, (80, 256), 0)

    def band(xx, mm):
        spot = xx * 8 + mm
        rows = pl.ds(pl.multiple_of(spot * 80, 80), 80)
        own = jnp.concatenate([qbuf[0, rows, :], qbuf[1, rows, :]], axis=1)
        wide = [
            jnp.where((row >= q4 * 20) & (row < q4 * 20 + 20), own, 0.0).astype(BF) for q4 in range(4)
        ]
        return dot(jnp.concatenate(wide, axis=1), wq[spot].reshape(1024, 128)).astype(BF)

    def block(xx, mm, sx, sm):
        return remote(
            bsend.at[xx * 8 + mm], brecv.at[sx, sm], bs_sem.at[xx * 8 + mm], br_sem.at[sx * 8 + sm], at(xx, mm)
        )

    @pl.loop(1, 32)
    def _(d):
        xx, mm = (x + d // 8) % 4, (me + d) % 8
        bsend[xx * 8 + mm] = band(xx, mm)
        block(xx, mm, x, me).start()

    brecv[x, me] = band(x, me)

    @pl.loop(1, 32)
    def _(d):
        xx, mm = (x + d // 8) % 4, (me + d) % 8
        block(xx, mm, xx, mm).wait_recv()

    blocks = jnp.concatenate([brecv[xx].reshape(640, 128) for xx in range(4)], axis=1)
    for part in range(4):
        rhs[part * 640:(part + 1) * 640, :] = dot(blocks, order_ref[:, part * 256:(part + 1) * 256]).astype(BF)

    def finish(mm):
        return (dot(lhs[mm], rhs[...]) * scale[mm]).astype(BF)

    @pl.loop(1, 8)
    def _(d):
        mm = (me + d) % 8
        osend[mm] = finish(mm)
        remote(osend.at[mm], o_ref.at[me], os_sem.at[mm], or_sem.at[me], at(x, mm)).start()

    o_ref[me] = finish(me)

    @pl.loop(1, 8)
    def _(d):
        mm = (me + d) % 8
        remote(osend.at[mm], o_ref.at[mm], os_sem.at[mm], or_sem.at[mm], at(x, mm)).wait()

    for d in range(1, 4):
        xx = (x + d) % 4
        remote(ksend.at[xx], krecv.at[x], ks_sem.at[xx], kr_sem.at[x], at(xx, me)).wait_send()
        remote(ph.at[x], ph.at[x], ps_sem.at[xx], pr_sem.at[x], at(xx, me)).wait_send()
        remote(win.at[x], win.at[x], ns_sem.at[xx], nr_sem.at[x], at(xx, me)).wait_send()
    for d in range(1, 8):
        mm = (me + d) % 8
        remote(modes_ref.at[mm], mrecv.at[me], ms_sem.at[mm], mr_sem.at[me], at(x, mm)).wait_send()
    for way in range(2):
        for step in range(hops[way]):
            for part in range(2):
                hop(way, step, part).wait_send()

    @pl.loop(1, 32)
    def _(d):
        xx, mm = (x + d // 8) % 4, (me + d) % 8
        block(xx, mm, x, me).wait_send()


def shards(g_wann, rot_k, qpoints, rot_kq, win_count, win_start, modes_vec, frequencies):
    nz = lax.axis_size("pb") // NX
    lattice, shift, spread, pick, mask, order = constants(nz)

    signs = jnp.stack([jnp.stack([rot_k[0], rot_k[1]], 1), jnp.stack([-rot_k[1], rot_k[0]], 1)])
    base = signs.reshape(2, 32, 2, 4, 2).transpose(0, 1, 3, 2, 4)
    base = jnp.broadcast_to(base[..., None], (2, 32, 4, 2, 2, 32)).reshape(64, 512)

    qm = qpoints.reshape(3, 8, 2, 4).transpose(2, 1, 3, 0).reshape(64, 3).astype(BF)
    qm = jnp.pad(qm, ((0, 0), (0, 125)))

    rotq = rot_kq.reshape(8, 2, 4, 2, 32, 32).transpose(0, 1, 4, 2, 3, 5).reshape(8, 64, 256)

    own = 1.0 / jnp.sqrt(2.0 * frequencies)
    high = lax.reduce_precision(own, 8, 7)
    middle = lax.reduce_precision(own - high, 8, 7)
    low = own - high - middle
    parts = jnp.stack([high, middle, low], axis=-1).astype(BF)
    modes = jnp.concatenate(
        [
            modes_vec[:, 0, :, :128], modes_vec[:, 1, :, :128],
            modes_vec[:, 0, :, 128:], modes_vec[:, 1, :, 128:], parts,
            jnp.zeros((64, 18, 93), BF),
        ],
        axis=-1,
    ).reshape(8, 144, 384)

    vmem = pl.BlockSpec(memory_space=pltpu.VMEM)
    smem = pl.BlockSpec(memory_space=pltpu.SMEM)
    sem = pltpu.SemaphoreType.DMA
    out = pl.pallas_call(
        functools.partial(kernel, nz),
        out_shape=jax.ShapeDtypeStruct((8, 144, 256), BF),
        in_specs=[smem, smem] + [vmem] * 11,
        out_specs=vmem,
        scratch_shapes=[
            pltpu.VMEM((128, 2048), BF),
            pltpu.VMEM((2048, 512), BF),
            pltpu.VMEM((4, 80, 128), F32),
            pltpu.VMEM((4, 80, 128), BF),
            pltpu.VMEM((4, 80, 128), BF),
            pltpu.VMEM((4, 80, 128), F32),
            pltpu.VMEM((288, 128), F32),
            pltpu.VMEM((nz, 288, 128), BF),
            pltpu.VMEM((4, 128, nz * 16), BF),
            pltpu.VMEM((4, 2, 256, 128), BF),
            pltpu.VMEM((32, 4, 256, 128), BF),
            pltpu.VMEM((2, 2560, 128), F32),
            pltpu.VMEM((32, 80, 128), BF),
            pltpu.VMEM((4, 8, 80, 128), BF),
            pltpu.VMEM((8, 144, 384), BF),
            pltpu.VMEM((8, 144, 2560), BF),
            pltpu.VMEM((8, 144, 256), F32),
            pltpu.VMEM((2560, 256), BF),
            pltpu.VMEM((8, 144, 256), BF),
            sem((4,)), sem((4,)), sem((4,)), sem((4,)), sem((4,)), sem((4,)), sem((8,)), sem((8,)),
            sem((2, 8, 2)), sem((2, 8, 2)), sem((32,)), sem((32,)), sem((8,)), sem((8,)),
        ],
        compiler_params=pltpu.CompilerParams(
            collective_id=0, has_side_effects=True, vmem_limit_bytes=56 * 1024 * 1024
        ),
    )(win_start, win_count, g_wann, base, qm, rotq, modes, lattice, shift, spread, pick, mask, order)
    return out.reshape(64, 18, 2, 128).transpose(0, 2, 1, 3)


def solution(mesh):
    placed = (
        P("pb", None, "mode", None),
        P(),
        P(None, "pb"),
        P("pb", None, None, None),
        P("pb"),
        P("pb"),
        P("pb", None, "mode", None),
        P("pb", "mode"),
    )
    return jax.shard_map(
        shards, mesh=mesh, in_specs=placed, out_specs=P("pb", None, "mode", None), check_vma=False
    )
```

time: 290 us -> 102 us (0.35)
  waiting for transfers between devices: 126 us -> 0 us
  Pallas kernels: 0 us -> 78.5 us
  matrix products: 40.9 us -> 0 us
  local copies, waits for them, and re-layouts: 53.6 us -> 22.8 us
  starting transfers between devices: 27.1 us -> 0 us
  between operations: 13.8 us -> 0.15 us
  blocking collectives: 13.6 us -> 0 us
  other arithmetic: 13.5 us -> 0.75 us
    all_gather x1 -> x0, waiting for transfers between devices: 117 us -> none  [shards(): all_k = lax.all_gather(k_side, 'pb', axis=0, tiled=True)]
    pallas_call x0 -> x1, Pallas kernels: none -> 78.5 us  [shards(): pl.pallas_call(functools.partial(kernel, nz), out_shape=jax.ShapeDtypeStr...]
    dot_general x14 -> x0, matrix products: 40.9 us -> none  [the longest x4 29.2 us: rotate_band(): jnp.einsum('qim,qcib->qcmb', first_op, second_op, preferred_element_type=...]
    all_to_all x3 -> x0, starting transfers between devices: 27.1 us -> none  [the longest x1 12.8 us: shards(): lax.all_to_all(modes_vec, 'mode', split_axis=0, concat_axis=2, tiled=True)]
    squeeze x2 -> x0, local copies, waits for them, and re-layouts: 14 us -> none  [the longest x1 7.29 us: shards(): q_grid[:, 1]]
    all_to_all x1 -> x0, blocking collectives: 13.6 us -> none  [shards(): lax.all_to_all(finished, 'mode', split_axis=2, concat_axis=0, tiled=True)]
    all_gather x1 -> x0, local copies, waits for them, and re-layouts: 12.3 us -> none  [shards(): all_k = lax.all_gather(k_side, 'pb', axis=0, tiled=True)]
    gather x2 -> x0, other arithmetic: 10 us -> none  [the longest x1 5.05 us: shards(): starts_q = jnp.repeat(win_start, QB, total_repeat_length=q_local)]
  transfers between devices with their start and end apart: 4 -> 0, of which waited for: 3 -> 0; matrix products, arithmetic and copies ran while one was open for 33% -> 0% of each run, Pallas kernels for 0% -> 0%
where the time goes in v1:
time: 102 us
  Pallas kernels  78.5 us (77%)
  local copies, waits for them, and re-layouts  22.8 us (22%)
    pallas_call x1, Pallas kernels, shards(): pl.pallas_call(functools.partial(kernel, nz), out_shape=jax.ShapeDtypeStr...  78.5 us
    slice x1, local copies, waits for them, and re-layouts, shards(): modes_vec[:, 1, :, :128]  4.59 us
    unnamed x12, local copies, waits for them, and re-layouts  3.49 us
    slice x1, local copies, waits for them, and re-layouts, shards(): modes_vec[:, 1, :, 128:]  3.41 us
    concatenate x5, local copies, waits for them, and re-layouts, shards(): jnp.concatenate([modes_vec[:, 0, :, :128], modes_vec[:, 1, :, :128], mode...  2.72 us
    reshape x1, local copies, waits for them, and re-layouts, shards(): return out.reshape(64, 18, 2, 128).transpose(0, 2, 1, 3)  2.47 us

profile of v1, /device:TPU:1, one launch (start us, length us, event | category | flops | bytes accessed | tf_op | source)
XLA Modules:
  0.0 102.1 jit_solution(4507386784934564346)
XLA Ops:
  0.0 0.7 fusion
  0.7 0.1 copy.28
  0.8 0.3 stack.34
  1.1 0.1 copy.29
  1.2 0.3 stack.35
  1.5 0.1 copy.30
  1.6 0.3 stack.36
  1.8 4.6 %slice_reduce_fusion.2 = (bf16[64,18,128]{2,1,0:T(8,128)(2,1)S(1)}, bf16[64,18,128]{2,1,0:T(8,128)(2,1)S(1)}) fusion(bf16[64,2,18,144]{3,1,2,0:T(2,128)(2,1)} %param.20), kind=kLoop, calls=%fused_computation.2 | loop fusion | bytes 1179648 | tf_op jit(solution)/shard_map/slice | solution.py:324
  6.4 0.0 copy-start
  6.4 0.1 concatenate.18
  6.5 0.1 concatenate.19
  6.6 1.1 %copy-done = bf16[64,2,18,144]{3,1,2,0:T(2,128)(2,1)S(1)} copy-done((bf16[64,2,18,144]{3,1,2,0:T(2,128)(2,1)S(1)}, bf16[64,2,18,144]{3,1,2,0:T(2,128)(2,1)}, u32[]{:S(2)}) %copy-start) | copy-done | bytes 663576
  7.7 3.4 %slice_reduce_fusion = (bf16[64,18,16]{2,1,0:T(8,128)(2,1)S(1)}, bf16[64,18,16]{2,1,0:T(8,128)(2,1)S(1)}) fusion(bf16[64,2,18,144]{3,1,2,0:T(2,128)(2,1)S(1)} %copy-done), kind=kLoop, calls=%fused_computation | loop fusion | bytes 147456 | tf_op jit(solution)/shard_map/slice | solution.py:325
  11.1 0.1 reshape.64
  11.2 0.1 reshape.65
  11.4 0.0 copy-start.3
  11.4 2.3 %concatenate.22.modes_ref = bf16[8,144,384]{2,1,0:T(8,128)(2,1)} concatenate(bf16[8,144,128]{2,1,0:T(8,128)(2,1)S(1)} %concatenate.18, bf16[8,144,128]{2,1,0:T(8,128)(2,1)S(1)} %concatenate.19, bf16[8,144,16]{2,1,0:T(8,128)(2,1)S(1)} %reshape.64, bf16[8,144,16]{2,1,0:T(8,128)(2,1)S(1)} %reshape.65, bf16[8,144,1]{2,1,0:T(8,128)(2,1)S(1)} %stack.34, bf16[8,144,1]{2,1,0:T(8,128)(2,1)S(1)} %stack.35, ...), dimensions={2} | concatenate | bytes 1769472 | tf_op jit(solution)/shard_map/concatenate | solution.py:322
  13.7 0.0 copy-done.3
  13.7 0.0 copy-start.1
  13.7 0.2 copy.22
  13.9 0.6 broadcast_in_dim.4
  14.6 0.8 reshape.60.base_ref
  15.4 0.0 copy-done.1
  15.4 1.6 %copy.24 = bf16[64,2,32,32]{3,2,1,0:T(8,128)(2,1)S(1)} copy(bf16[64,2,32,32]{0,3,2,1:T(8,128)(2,1)S(1)} %copy-done.1) | data formatting | bytes 524288 | tf_op args[3]
  17.0 1.0 copy.25
  18.0 0.0 copy-start.2
  18.0 0.0 copy-start.4
  18.0 1.4 %reshape.62.rotq_ref = bf16[8,64,256]{2,1,0:T(8,128)(2,1)} reshape(bf16[8,2,32,4,2,32]{5,4,3,2,1,0:T(2,128)(2,1)S(1)} %copy.25) | data formatting | bytes 524288 | tf_op jit(solution)/shard_map/reshape | solution.py:315
  19.4 0.0 copy-done.2
  19.4 0.8 copy.36.g_ref
  20.3 0.0 copy-done.4
  20.3 0.1 convert_element_type.17
  20.4 0.2 copy.23
  20.6 0.6 pad.4.qm_ref
  21.2 78.5 %shard_map.136 = bf16[8,144,256]{2,1,0:T(8,128)(2,1)} custom-call(s32[8]{0:T(128)} %ws_ref.1, s32[8]{0:T(128)} %wc_ref.1, bf16[4,2,18,1024]{3,2,1,0:T(8,128)(2,1)} %copy.36.g_ref, bf16[64,512]{1,0:T(8,128)(2,1)} %reshape.60.base_ref, bf16[64,128]{1,0:T(8,128)(2,1)} %pad.4.qm_ref, bf16[8,64,256]{2,1,0:T(8,128)(2,1)} %reshape.62.rotq_ref, ...), custom_call_target="tpu_custom_call" | custom-call | tf_op jit(solution)/shard_map/pallas_call | solution.py:334
  99.7 2.5 %reshape.63 = bf16[64,18,2,128]{3,2,1,0:T(2,128)(2,1)} reshape(bf16[8,144,256]{2,1,0:T(8,128)(2,1)} %shard_map.136) | data formatting | bytes 1179648 | tf_op jit(solution)/shard_map/reshape | solution.py:366
  (5 shorter events, 0.1 us)
Async XLA Ops:
  6.4 1.3 %copy-start = (bf16[64,2,18,144]{3,1,2,0:T(2,128)(2,1)S(1)}, bf16[64,2,18,144]{3,1,2,0:T(2,128)(2,1)}, u32[]{:S(2)}) copy-start(bf16[64,2,18,144]{3,1,2,0:T(2,128)(2,1)} %param.20) | copy-start | bytes 1990660
  11.4 2.3 %copy-start.3 = (bf16[2,32,8]{1,2,0:T(8,128)(2,1)S(1)}, bf16[2,32,8]{1,2,0:T(8,128)(2,1)}, u32[]{:S(2)}) copy-start(bf16[2,32,8]{1,2,0:T(8,128)(2,1)} %param.15) | copy-start | bytes 3076
  13.7 1.7 %copy-start.1 = (bf16[64,2,32,32]{0,3,2,1:T(8,128)(2,1)S(1)}, bf16[64,2,32,32]{0,3,2,1:T(8,128)(2,1)}, u32[]{:S(2)}) copy-start(bf16[64,2,32,32]{0,3,2,1:T(8,128)(2,1)} %param.17) | copy-start | bytes 786436
  18.0 1.4 %copy-start.2 = (bf16[4,2,18,1024]{3,1,2,0:T(2,128)(2,1)S(1)}, bf16[4,2,18,1024]{3,1,2,0:T(2,128)(2,1)}, u32[]{:S(2)}) copy-start(bf16[4,2,18,1024]{3,1,2,0:T(2,128)(2,1)} %param.14) | copy-start | bytes 884740
  18.0 2.3 %copy-start.4 = (s32[3,64]{1,0:T(4,128)S(1)}, s32[3,64]{1,0:T(4,128)}, u32[]{:S(2)}) copy-start(s32[3,64]{1,0:T(4,128)} %param.16) | copy-start | bytes 2308

commit v2 on v1

--- a/solution.py
+++ b/solution.py
@@ -9,6 +9,7 @@
 
 NX = 4
 NM = 8
+PARTS = 3
 TWO_PI = 6.283185307179586
 BF = jnp.bfloat16
 F32 = jnp.float32
@@ -16,6 +17,10 @@
 
 def dot(a, b):
     return jnp.dot(a, b, preferred_element_type=F32)
+
+
+def dot_t(a, b):
+    return lax.dot_general(a, b, (((1,), (1,)), ((), ())), preferred_element_type=F32)
 
 
 def constants(nz):
@@ -42,13 +47,11 @@
                     spread[par, q4, 0, m, q4, 1, b, par, 1, m, b] = 1
     spread = spread.reshape(2, 128, 2048)
 
-    pick = np.zeros((384, 1536), np.float32)
+    pick = np.zeros((288, 1280), np.float32)
     for ri in range(2):
         for c in range(144):
-            source = ri * 128 + c if c < 128 else 256 + ri * 16 + c - 128
             for q4 in range(4):
-                pick[source, ri * 640 + c // 18 * 80 + q4 * 20 + c % 18] = 1
-    pick[288:291, 1280:] = 1
+                pick[ri * 144 + c, ri * 640 + c // 18 * 80 + q4 * 20 + c % 18] = 1
     mask = np.zeros((2, 2, 4, 18, 8, 4, 20), np.float32)
     for par in range(2):
         for q4 in range(4):
@@ -65,15 +68,34 @@
                     order[xx, par, 1, m, b, par, 1, 0, m, xx * 2 + b] = -1
                     order[xx, par, 0, m, b, par, 1, 1, m, xx * 2 + b] = 1
     order = order.reshape(512, 1024)
+
+    bands = np.zeros((128, 4, 2, 2, 32), np.float32)
+    for xx in range(4):
+        for b in range(2):
+            bands[xx * 2 + b, xx, :, b, :] = 1
+    bands = bands.reshape(128, 512)
+
+    q = np.arange(64)
+    first = np.zeros((64, 128), np.float32)
+    first[q, q // 4 % 8 * 8 + q // 32 * 4 + q % 4] = 1
+    second = np.zeros((64, 64), np.float32)
+    second[q, q // 2 % 8 * 8 + q % 2 * 4 + q // 16] = 1
+
+    modes = np.zeros((144, 24), np.float32)
+    modes[np.arange(144), np.arange(144) % 18] = 1
     half = lambda a: jnp.asarray(a, BF)
-    return half(lattice), jnp.asarray(shift), half(spread), half(pick), half(mask), half(order)
+    small = [half(lattice), jnp.asarray(shift), half(bands), half(first), half(second), half(modes)]
+    return small, [half(spread), half(pick), half(mask), half(order)]
 
 
 def kernel(
-    nz, ws_ref, wc_ref, g_ref, base_ref, qm_ref, rotq_ref, modes_ref,
-    lattice_ref, shift_ref, spread_ref, pick_ref, mask_ref, order_ref, o_ref,
-    gl, kw, kf, ksend, krecv, kx, ka, kbuf, ph, win, wq, qbuf, bsend, brecv, mrecv, lhs, scale, rhs, osend,
-    ks_sem, kr_sem, ps_sem, pr_sem, ns_sem, nr_sem, ms_sem, mr_sem, zs_sem, zr_sem, bs_sem, br_sem, os_sem, or_sem,
+    nz, ws_ref, wc_ref, g_ref, rot_ref, qp_ref, rotq_ref, freq_ref, modes_ref,
+    lattice_ref, shift_ref, bands_ref, first_ref, second_ref, rowmode_ref, spread_in, pick_in, mask_in, order_in, o_ref,
+    spread_ref, pick_ref, mask_ref, order_ref,
+    gf, gl, kw, tf, kf, ksend, krecv, kx, ka, kbuf, ph, xf, win, wq, qbuf, bsend, brecv, mrecv, frecv, lhs, scale, rhs,
+    of, osend, c_sem,
+    ks_sem, kr_sem, ps_sem, pr_sem, ns_sem, nr_sem, ms_sem, mr_sem, fs_sem, fr_sem, zs_sem, zr_sem, bs_sem, br_sem,
+    os_sem, or_sem,
 ):
     me = lax.axis_index("mode")
     pb = lax.axis_index("pb")
@@ -104,22 +126,38 @@
         pl.semaphore_signal(barrier, inc=1, device_id=left, device_id_type=pl.DeviceIdType.MESH)
         pl.semaphore_signal(barrier, inc=1, device_id=right, device_id_type=pl.DeviceIdType.MESH)
 
-    lane_i = lax.broadcasted_iota(jnp.int32, (32, 512), 1) % 32
+    constant = [
+        pltpu.make_async_copy(source, held, c_sem.at[n])
+        for n, (source, held) in enumerate(
+            ((spread_in, spread_ref), (pick_in, pick_ref), (mask_in, mask_ref), (order_in, order_ref))
+        )
+    ]
+    for copy in constant:
+        copy.start()
+
+    lane = lax.broadcasted_iota(jnp.int32, (32, 512), 1)
+    lane_i = lane % 32
+    real = dot(rot_ref[0], bands_ref[...])
+    imag = dot(rot_ref[1], bands_ref[...])
+    in_real = lane % 128 < 64
+    parts = (jnp.where(in_real, real, imag).astype(BF), jnp.where(in_real, -imag, real).astype(BF))
     for ri in range(2):
-        part = base_ref[ri * 32:(ri + 1) * 32, :]
+        part = parts[ri]
 
         @pl.loop(0, 32)
         def _(i):
             kw[pl.ds(pl.multiple_of(ri * 1024 + i * 32, 32), 32), :] = jnp.where(lane_i == i, part, 0.0).astype(BF)
 
-    for r in range(4):
-        for ri in range(2):
-            gl[r * 32:r * 32 + 18, ri * 1024:(ri + 1) * 1024] = g_ref[r, ri]
-    turned = dot(gl[...], kw[...])
+    gf[...] = g_ref[...].astype(F32)
+    for ri in range(2):
+        for k in range(8):
+            block = (ri * 8 + k) * 128
+            gl[0:72, block:block + 128] = gf[pl.ds(k * 2 + ri, 72, stride=16), :].astype(BF)
+    tf[...] = dot(gl[...], kw[...])
     kf[...] = jnp.zeros_like(kf)
     for xx in range(4):
         for r in range(4):
-            kf[xx, pl.ds(r, 18, stride=4), :] = turned[r * 32:r * 32 + 18, xx * 128:(xx + 1) * 128]
+            kf[xx, pl.ds(r, 18, stride=4), :] = tf[r * 18:r * 18 + 18, xx * 128:(xx + 1) * 128]
     ksend[...] = kf[...].astype(BF)
 
     pl.semaphore_wait(barrier, 31 + (2 if nz > 1 else 0))
@@ -129,28 +167,22 @@
         remote(ksend.at[xx], krecv.at[x], ks_sem.at[xx], kr_sem.at[x], at(xx, me)).start()
     krecv[x] = ksend[x]
 
-    inner = dot(qm_ref[...], lattice_ref[...]).astype(jnp.int32) & 31
+    def rows_of(mm):
+        return modes_ref.at[pl.ds(pl.multiple_of(mm * 144, 144), 144)]
+
+    for d in range(1, 8):
+        mm = (me + d) % 8
+        remote(rows_of(mm), mrecv.at[me], ms_sem.at[mm], mr_sem.at[me], at(x, mm)).start()
+        remote(freq_ref, frecv.at[me], fs_sem.at[mm], fr_sem.at[me], at(x, mm)).start()
+    own_modes = pltpu.make_async_copy(rows_of(me), mrecv.at[me], c_sem.at[4])
+    own_modes.start()
+    frecv[me] = freq_ref[...]
+
+    points = dot_t(first_ref[...], qp_ref[...]).astype(BF)
+    inner = dot(points, lattice_ref[...]).astype(jnp.int32) & 31
     angle = inner.astype(F32) * (TWO_PI / 32)
     ph[x, 0:64, :] = jnp.cos(angle).astype(BF)
     ph[x, 64:128, :] = jnp.sin(angle).astype(BF)
-    for d in range(1, 4):
-        xx = (x + d) % 4
-        remote(ph.at[x], ph.at[x], ps_sem.at[xx], pr_sem.at[x], at(xx, me)).start()
-
-    for d in range(1, 8):
-        mm = (me + d) % 8
-        remote(modes_ref.at[mm], mrecv.at[me], ms_sem.at[mm], mr_sem.at[me], at(x, mm)).start()
-    mrecv[me] = modes_ref[me]
-
-    lane_m = lax.broadcasted_iota(jnp.int32, (256, 128), 1) % 16
-    for t in range(8):
-        chosen = jnp.where((shift_ref[...] == ws_ref[t]) & (lane_m < wc_ref[t]), 1.0, 0.0).astype(BF)
-        cut = dot(rotq_ref[t], chosen).astype(BF)
-        win[x, 0, t * 32:(t + 1) * 32, :] = cut[0:32]
-        win[x, 1, t * 32:(t + 1) * 32, :] = cut[32:64]
-    for d in range(1, 4):
-        xx = (x + d) % 4
-        remote(win.at[x], win.at[x], ns_sem.at[xx], nr_sem.at[x], at(xx, me)).start()
 
     for d in range(1, 4):
         xx = (x + d) % 4
@@ -163,10 +195,42 @@
 
     def hop(way, step, part):
         shard = (z + (nz - step if way == 0 else step)) % nz
-        piece = kbuf.at[shard, pl.ds(part * 144, 144)]
+        piece = kbuf.at[shard, pl.ds(part * (288 // PARTS), 288 // PARTS)]
         return remote(piece, piece, zs_sem.at[way, step, part], zr_sem.at[way, step, part], right if way == 0 else left)
 
     hops = (nz // 2, nz - 1 - nz // 2)
+
+    def advance(step):
+        for part in range(PARTS):
+            for way in range(2):
+                if step < hops[way]:
+                    if step > 0:
+                        hop(way, step - 1, part).wait_recv()
+                    hop(way, step, part).start()
+
+    advance(0)
+    for d in range(1, 4):
+        xx = (x + d) % 4
+        remote(ph.at[x], ph.at[x], ps_sem.at[xx], pr_sem.at[x], at(xx, me)).start()
+
+    @pl.loop(0, 32)
+    def _(i):
+        both = [rotq_ref[pl.ds(pl.multiple_of(ri * 1024 + i * 32, 32), 32), :] for ri in range(2)]
+        flipped = dot_t(second_ref[...], jnp.concatenate(both, axis=0))
+        for q4 in range(4):
+            xf[q4, pl.ds(i, 16, stride=32), :] = flipped[q4 * 16:(q4 + 1) * 16]
+
+    lane_m = lax.broadcasted_iota(jnp.int32, (256, 128), 1) % 16
+    for t in range(8):
+        chosen = jnp.where((shift_ref[...] == ws_ref[t]) & (lane_m < wc_ref[t]), 1.0, 0.0).astype(BF)
+        cut = jnp.zeros((64, 128), F32)
+        for q4 in range(4):
+            cut = cut + dot(xf[q4, t * 64:(t + 1) * 64, :].astype(BF), chosen[q4 * 64:(q4 + 1) * 64])
+        win[x, 0, t * 32:(t + 1) * 32, :] = cut[0:32].astype(BF)
+        win[x, 1, t * 32:(t + 1) * 32, :] = cut[32:64].astype(BF)
+    for d in range(1, 4):
+        xx = (x + d) % 4
+        remote(win.at[x], win.at[x], ns_sem.at[xx], nr_sem.at[x], at(xx, me)).start()
 
     def weights(xx):
         for par in range(2):
@@ -177,10 +241,18 @@
                     start = par * 128 + g * 32
                     wq[pl.ds(xx * 8, 8), q4, start:start + 32, :] = rows
 
+    row_q = sum((lax.broadcasted_iota(jnp.int32, (144, 128), 0) >= 18 * n).astype(jnp.int32) for n in range(1, 8))
+    diagonal = lax.broadcasted_iota(jnp.int32, (144, 128), 1) == row_q + me * 8
+
     def vectors(mm):
-        spreaded = dot(mrecv[mm], pick_ref[...])
-        scale[mm] = spreaded[:, 1280:]
-        both = spreaded[:, :1280].astype(BF)
+        own = 1.0 / jnp.sqrt(2.0 * frecv[mm])
+        high = own.astype(BF)
+        rest = own - high.astype(F32)
+        middle = rest.astype(BF)
+        low = (rest - middle.astype(F32)).astype(BF)
+        by_row = dot(rowmode_ref[...], high) + dot(rowmode_ref[...], middle) + dot(rowmode_ref[...], low)
+        scale[mm] = jnp.sum(jnp.where(diagonal, by_row, 0.0), axis=1, keepdims=True)
+        both = dot(mrecv[mm], pick_ref[...]).astype(BF)
         for par in range(2):
             for ri in range(2):
                 start = (par * 2 + ri) * 640
@@ -190,15 +262,17 @@
         remote(win.at[xx], win.at[xx], ns_sem.at[xx], nr_sem.at[xx], at(xx, me)).wait_recv()
 
     def wait_vectors(mm):
-        remote(modes_ref.at[mm], mrecv.at[mm], ms_sem.at[mm], mr_sem.at[mm], at(x, mm)).wait_recv()
+        remote(rows_of(mm), mrecv.at[mm], ms_sem.at[mm], mr_sem.at[mm], at(x, mm)).wait_recv()
+        remote(freq_ref, frecv.at[mm], fs_sem.at[mm], fr_sem.at[mm], at(x, mm)).wait_recv()
 
     for step in range(8):
-        for part in range(2):
-            for way in range(2):
-                if step < hops[way]:
-                    if step > 0:
-                        hop(way, step - 1, part).wait_recv()
-                    hop(way, step, part).start()
+        if step > 0:
+            advance(step)
+        else:
+            constant[0].wait()
+            constant[1].wait()
+            constant[2].wait()
+            own_modes.wait()
         if step < 4:
             xx = (x + step) % 4
             if step > 0:
@@ -210,7 +284,7 @@
         vectors(mm)
     for way in range(2):
         if hops[way]:
-            for part in range(2):
+            for part in range(PARTS):
                 hop(way, hops[way] - 1, part).wait_recv()
 
     for d in range(1, 4):
@@ -262,12 +336,16 @@
         xx, mm = (x + d // 8) % 4, (me + d) % 8
         block(xx, mm, xx, mm).wait_recv()
 
+    constant[3].wait()
     blocks = jnp.concatenate([brecv[xx].reshape(640, 128) for xx in range(4)], axis=1)
     for part in range(4):
         rhs[part * 640:(part + 1) * 640, :] = dot(blocks, order_ref[:, part * 256:(part + 1) * 256]).astype(BF)
 
     def finish(mm):
-        return (dot(lhs[mm], rhs[...]) * scale[mm]).astype(BF)
+        done = dot(lhs[mm], rhs[...]) * scale[mm]
+        for ri in range(2):
+            of[pl.ds(ri, 144, stride=2), :] = done[:, ri * 128:(ri + 1) * 128]
+        return of[...].astype(BF)
 
     @pl.loop(1, 8)
     def _(d):
@@ -289,10 +367,11 @@
         remote(win.at[x], win.at[x], ns_sem.at[xx], nr_sem.at[x], at(xx, me)).wait_send()
     for d in range(1, 8):
         mm = (me + d) % 8
-        remote(modes_ref.at[mm], mrecv.at[me], ms_sem.at[mm], mr_sem.at[me], at(x, mm)).wait_send()
+        remote(rows_of(mm), mrecv.at[me], ms_sem.at[mm], mr_sem.at[me], at(x, mm)).wait_send()
+        remote(freq_ref, frecv.at[me], fs_sem.at[mm], fr_sem.at[me], at(x, mm)).wait_send()
     for way in range(2):
         for step in range(hops[way]):
-            for part in range(2):
+            for part in range(PARTS):
                 hop(way, step, part).wait_send()
 
     @pl.loop(1, 32)
@@ -303,42 +382,33 @@
 
 def shards(g_wann, rot_k, qpoints, rot_kq, win_count, win_start, modes_vec, frequencies):
     nz = lax.axis_size("pb") // NX
-    lattice, shift, spread, pick, mask, order = constants(nz)
-
-    signs = jnp.stack([jnp.stack([rot_k[0], rot_k[1]], 1), jnp.stack([-rot_k[1], rot_k[0]], 1)])
-    base = signs.reshape(2, 32, 2, 4, 2).transpose(0, 1, 3, 2, 4)
-    base = jnp.broadcast_to(base[..., None], (2, 32, 4, 2, 2, 32)).reshape(64, 512)
-
-    qm = qpoints.reshape(3, 8, 2, 4).transpose(2, 1, 3, 0).reshape(64, 3).astype(BF)
-    qm = jnp.pad(qm, ((0, 0), (0, 125)))
-
-    rotq = rot_kq.reshape(8, 2, 4, 2, 32, 32).transpose(0, 1, 4, 2, 3, 5).reshape(8, 64, 256)
-
-    own = 1.0 / jnp.sqrt(2.0 * frequencies)
-    high = lax.reduce_precision(own, 8, 7)
-    middle = lax.reduce_precision(own - high, 8, 7)
-    low = own - high - middle
-    parts = jnp.stack([high, middle, low], axis=-1).astype(BF)
-    modes = jnp.concatenate(
-        [
-            modes_vec[:, 0, :, :128], modes_vec[:, 1, :, :128],
-            modes_vec[:, 0, :, 128:], modes_vec[:, 1, :, 128:], parts,
-            jnp.zeros((64, 18, 93), BF),
-        ],
-        axis=-1,
-    ).reshape(8, 144, 384)
+    small, large = constants(nz)
+
+    g_rows = g_wann.reshape(4, 2, 18, 8, 128).transpose(0, 2, 3, 1, 4).reshape(1152, 128)
+    rot = jnp.pad(rot_k, ((0, 0), (0, 0), (0, 120)))
+    points = jnp.pad(qpoints.astype(BF), ((0, 125), (0, 64)))
+    rotq = rot_kq.transpose(1, 2, 3, 0).reshape(2048, 64)
+    freq = jnp.pad(frequencies.T, ((0, 6), (0, 64)), constant_values=1.0)
+    modes = modes_vec.transpose(0, 2, 1, 3).reshape(1152, 288)
 
     vmem = pl.BlockSpec(memory_space=pltpu.VMEM)
     smem = pl.BlockSpec(memory_space=pltpu.SMEM)
+    whole = pl.BlockSpec(memory_space=pl.ANY)
     sem = pltpu.SemaphoreType.DMA
     out = pl.pallas_call(
         functools.partial(kernel, nz),
-        out_shape=jax.ShapeDtypeStruct((8, 144, 256), BF),
-        in_specs=[smem, smem] + [vmem] * 11,
+        out_shape=jax.ShapeDtypeStruct((8, 288, 128), BF),
+        in_specs=[smem, smem] + [vmem] * 12 + [whole] * 4,
         out_specs=vmem,
         scratch_shapes=[
-            pltpu.VMEM((128, 2048), BF),
+            pltpu.VMEM((2, 128, 2048), BF),
+            pltpu.VMEM((288, 1280), BF),
+            pltpu.VMEM((2, 144, 640), BF),
+            pltpu.VMEM((512, 1024), BF),
+            pltpu.VMEM((1152, 128), F32),
+            pltpu.VMEM((80, 2048), BF),
             pltpu.VMEM((2048, 512), BF),
+            pltpu.VMEM((80, 512), F32),
             pltpu.VMEM((4, 80, 128), F32),
             pltpu.VMEM((4, 80, 128), BF),
             pltpu.VMEM((4, 80, 128), BF),
@@ -346,23 +416,27 @@
             pltpu.VMEM((288, 128), F32),
             pltpu.VMEM((nz, 288, 128), BF),
             pltpu.VMEM((4, 128, nz * 16), BF),
+            pltpu.VMEM((4, 512, 64), F32),
             pltpu.VMEM((4, 2, 256, 128), BF),
             pltpu.VMEM((32, 4, 256, 128), BF),
             pltpu.VMEM((2, 2560, 128), F32),
             pltpu.VMEM((32, 80, 128), BF),
             pltpu.VMEM((4, 8, 80, 128), BF),
-            pltpu.VMEM((8, 144, 384), BF),
+            pltpu.VMEM((8, 144, 288), BF),
+            pltpu.VMEM((8, 24, 128), F32),
             pltpu.VMEM((8, 144, 2560), BF),
-            pltpu.VMEM((8, 144, 256), F32),
+            pltpu.VMEM((8, 144, 1), F32),
             pltpu.VMEM((2560, 256), BF),
-            pltpu.VMEM((8, 144, 256), BF),
-            sem((4,)), sem((4,)), sem((4,)), sem((4,)), sem((4,)), sem((4,)), sem((8,)), sem((8,)),
-            sem((2, 8, 2)), sem((2, 8, 2)), sem((32,)), sem((32,)), sem((8,)), sem((8,)),
+            pltpu.VMEM((288, 128), F32),
+            pltpu.VMEM((8, 288, 128), BF),
+            sem((5,)),
+            sem((4,)), sem((4,)), sem((4,)), sem((4,)), sem((4,)), sem((4,)), sem((8,)), sem((8,)), sem((8,)), sem((8,)),
+            sem((2, 8, PARTS)), sem((2, 8, PARTS)), sem((32,)), sem((32,)), sem((8,)), sem((8,)),
         ],
         compiler_params=pltpu.CompilerParams(
             collective_id=0, has_side_effects=True, vmem_limit_bytes=56 * 1024 * 1024
         ),
-    )(win_start, win_count, g_wann, base, qm, rotq, modes, lattice, shift, spread, pick, mask, order)
+    )(win_start, win_count, g_rows, rot, points, rotq, freq, modes, *small, *large)
     return out.reshape(64, 18, 2, 128).transpose(0, 2, 1, 3)
 
 

time: 102 us -> 92.6 us (0.908)
  local copies, waits for them, and re-layouts: 22.8 us -> 9.56 us
  Pallas kernels: 78.5 us -> 82.1 us
    slice x3 -> x0, local copies, waits for them, and re-layouts: 8 us -> none  [the longest x1 4.59 us: shards(): modes_vec[:, 1, :, :128]]
    pallas_call x1, Pallas kernels: 78.5 us -> 82.1 us  [shards(): pl.pallas_call(functools.partial(kernel, nz), out_shape=jax.ShapeDtypeStr...]
    concatenate x5 -> x0, local copies, waits for them, and re-layouts: 2.72 us -> none  [shards(): jnp.concatenate([modes_vec[:, 0, :, :128], modes_vec[:, 1, :, :128], mode...]
    pad x1 -> x3, local copies, waits for them, and re-layouts: 0.62 us -> 2.53 us  [the longest x1 1.31 us: shards(): freq = jnp.pad(frequencies.T, ((0, 6), (0, 64)), constant_values=1.0)]
    transpose x2 -> x0, local copies, waits for them, and re-layouts: 1.17 us -> none  [the longest x1 0.98 us: shards(): rot_kq.reshape(8, 2, 4, 2, 32, 32).transpose(0, 1, 4, 2, 3, 5)]
    another operation x6 -> x0, local copies, waits for them, and re-layouts: 1.09 us -> none  [the longest x3 0.76 us: shards(): parts = jnp.stack([high, middle, low], axis=-1).astype(BF)]
    reshape x3 -> x1, local copies, waits for them, and re-layouts: 4.74 us -> 3.97 us  [shards(): modes = modes_vec.transpose(0, 2, 1, 3).reshape(1152, 288)]
    unnamed x12 -> x2, local copies, waits for them, and re-layouts: 3.49 us -> 3.06 us
where the time goes in v2:
time: 92.6 us; the launch traced here: 92.3 us
  Pallas kernels  82.1 us (89%)
  local copies, waits for them, and re-layouts  9.56 us (10%)
    pallas_call x1, Pallas kernels, shards(): pl.pallas_call(functools.partial(kernel, nz), out_shape=jax.ShapeDtypeStr...  82.1 us
    reshape x1, local copies, waits for them, and re-layouts, shards(): modes = modes_vec.transpose(0, 2, 1, 3).reshape(1152, 288)  3.97 us
    unnamed x2, local copies, waits for them, and re-layouts  3.06 us

profile of v2, /device:TPU:1, one launch (start us, length us, event | category | flops | bytes accessed | tf_op | source)
XLA Modules:
  0.0 92.3 jit_solution(10939618802084038303)
XLA Ops:
  0.0 0.7 convert_element_type.7
  0.7 1.3 %pad.14.freq_ref = f32[24,128]{1,0:T(8,128)} pad(f32[18,64]{1,0:T(8,128)} %bitcast.17, f32[]{:T(128)} %constant.24.clone.1), padding=0_6x0_64 | pad | bytes 16900 | tf_op jit(solution)/shard_map/jit(_pad)/pad | solution.py:391
  2.0 0.8 copy.22
  2.8 0.6 pad.12.rot_ref
  3.4 0.6 pad.13.qp_ref
  4.0 4.0 %reshape.18.modes_ref = bf16[1152,288]{1,0:T(8,128)(2,1)} reshape(bf16[64,18,2,144]{3,2,1,0:T(2,128)(2,1)} %bitcast.14) | data formatting | bytes 1327104 | tf_op jit(solution)/shard_map/reshape | solution.py:392
  8.0 82.1 %shard_map.172 = bf16[8,288,128]{2,1,0:T(8,128)(2,1)} custom-call(s32[8]{0:T(128)} %ws_ref.1, s32[8]{0:T(128)} %wc_ref.1, bf16[1152,128]{1,0:T(8,128)(2,1)} %bitcast.16, bf16[2,32,128]{2,1,0:T(8,128)(2,1)} %pad.12.rot_ref, bf16[128,128]{1,0:T(8,128)(2,1)} %pad.13.qp_ref, bf16[2048,64]{1,0:T(8,128)(2,1)} %bitcast.15, f32[24,128]{1,0:T(8,128)} %pad.14.freq_ref, ...), custom_call_target="tpu_custom_call" | custom-call | tf_op jit(solution)/shard_map/pallas_call | solution.py:398
  90.1 2.3 %copy.24 = bf16[64,2,18,128]{3,1,2,0:T(2,128)(2,1)} copy(bf16[64,2,18,128]{3,1,2,0:T(2,128)(2,1)} %bitcast.13) | data formatting | bytes 1179648

commit v3 on v2

--- a/solution.py
+++ b/solution.py
@@ -9,7 +9,6 @@
 
 NX = 4
 NM = 8
-PARTS = 3
 TWO_PI = 6.283185307179586
 BF = jnp.bfloat16
 F32 = jnp.float32
@@ -27,7 +26,7 @@
     rows = np.arange(nz * 16)
     z, x, r4 = rows // 16, rows // 4 % 4, rows % 4
     r = (x * nz + z) * 4 + r4
-    lattice = np.zeros((128, nz * 16), np.float32)
+    lattice = np.zeros((8, nz * 16), np.float32)
     lattice[0] = r % 8 - 4
     lattice[1] = r // 8 % 8 - 4
     lattice[2] = r // 64 - 4
@@ -69,11 +68,11 @@
                     order[xx, par, 0, m, b, par, 1, 1, m, xx * 2 + b] = 1
     order = order.reshape(512, 1024)
 
-    bands = np.zeros((128, 4, 2, 2, 32), np.float32)
+    bands = np.zeros((8, 4, 2, 2, 32), np.float32)
     for xx in range(4):
         for b in range(2):
             bands[xx * 2 + b, xx, :, b, :] = 1
-    bands = bands.reshape(128, 512)
+    bands = bands.reshape(8, 512)
 
     q = np.arange(64)
     first = np.zeros((64, 128), np.float32)
@@ -92,7 +91,7 @@
     nz, ws_ref, wc_ref, g_ref, rot_ref, qp_ref, rotq_ref, freq_ref, modes_ref,
     lattice_ref, shift_ref, bands_ref, first_ref, second_ref, rowmode_ref, spread_in, pick_in, mask_in, order_in, o_ref,
     spread_ref, pick_ref, mask_ref, order_ref,
-    gf, gl, kw, tf, kf, ksend, krecv, kx, ka, kbuf, ph, xf, win, wq, qbuf, bsend, brecv, mrecv, frecv, lhs, scale, rhs,
+    gf, gl, kw, tf, qs, fs, kf, ksend, krecv, kx, ka, kbuf, ph, xf, win, wq, qbuf, bsend, brecv, mrecv, frecv, lhs, scale, rhs,
     of, osend, c_sem,
     ks_sem, kr_sem, ps_sem, pr_sem, ns_sem, nr_sem, ms_sem, mr_sem, fs_sem, fr_sem, zs_sem, zr_sem, bs_sem, br_sem,
     os_sem, or_sem,
@@ -111,8 +110,8 @@
             device_id=where, device_id_type=pl.DeviceIdType.MESH,
         )
 
-    right = {"mode": me, "pb": x * nz + (z + 1) % nz}
-    left = {"mode": me, "pb": x * nz + (z + nz - 1) % nz}
+    def along_z(step):
+        return {"mode": me, "pb": x * nz + (z + nz + step) % nz}
 
     barrier = pltpu.get_barrier_semaphore()
 
@@ -122,9 +121,9 @@
             barrier, inc=1, device_id=at((x + d // 8) % 4, (me + d) % 8), device_id_type=pl.DeviceIdType.MESH
         )
 
-    if nz > 1:
-        pl.semaphore_signal(barrier, inc=1, device_id=left, device_id_type=pl.DeviceIdType.MESH)
-        pl.semaphore_signal(barrier, inc=1, device_id=right, device_id_type=pl.DeviceIdType.MESH)
+    near = (-3, 3, -1, 1, -2, 2)
+    for step in near:
+        pl.semaphore_signal(barrier, inc=1, device_id=along_z(step), device_id_type=pl.DeviceIdType.MESH)
 
     constant = [
         pltpu.make_async_copy(source, held, c_sem.at[n])
@@ -137,8 +136,10 @@
 
     lane = lax.broadcasted_iota(jnp.int32, (32, 512), 1)
     lane_i = lane % 32
-    real = dot(rot_ref[0], bands_ref[...])
-    imag = dot(rot_ref[1], bands_ref[...])
+    turn_b = lambda ri: lax.dot_general(
+        rot_ref[ri], bands_ref[...], (((0,), (0,)), ((), ())), preferred_element_type=F32
+    )
+    real, imag = turn_b(0), turn_b(1)
     in_real = lane % 128 < 64
     parts = (jnp.where(in_real, real, imag).astype(BF), jnp.where(in_real, -imag, real).astype(BF))
     for ri in range(2):
@@ -160,7 +161,7 @@
             kf[xx, pl.ds(r, 18, stride=4), :] = tf[r * 18:r * 18 + 18, xx * 128:(xx + 1) * 128]
     ksend[...] = kf[...].astype(BF)
 
-    pl.semaphore_wait(barrier, 31 + (2 if nz > 1 else 0))
+    pl.semaphore_wait(barrier, 31 + len(near))
 
     for d in range(1, 4):
         xx = (x + d) % 4
@@ -170,15 +171,19 @@
     def rows_of(mm):
         return modes_ref.at[pl.ds(pl.multiple_of(mm * 144, 144), 144)]
 
+    fs[...] = jnp.ones_like(fs)
+    fs[0:18, 0:64] = freq_ref[...]
     for d in range(1, 8):
         mm = (me + d) % 8
         remote(rows_of(mm), mrecv.at[me], ms_sem.at[mm], mr_sem.at[me], at(x, mm)).start()
-        remote(freq_ref, frecv.at[me], fs_sem.at[mm], fr_sem.at[me], at(x, mm)).start()
+        remote(fs, frecv.at[me], fs_sem.at[mm], fr_sem.at[me], at(x, mm)).start()
     own_modes = pltpu.make_async_copy(rows_of(me), mrecv.at[me], c_sem.at[4])
     own_modes.start()
-    frecv[me] = freq_ref[...]
-
-    points = dot_t(first_ref[...], qp_ref[...]).astype(BF)
+    frecv[me] = fs[...]
+
+    qs[...] = jnp.zeros_like(qs)
+    qs[0:3, 0:64] = qp_ref[...].astype(F32)
+    points = dot_t(first_ref[...], qs[...].astype(BF)).astype(BF)
     inner = dot(points, lattice_ref[...]).astype(jnp.int32) & 31
     angle = inner.astype(F32) * (TWO_PI / 32)
     ph[x, 0:64, :] = jnp.cos(angle).astype(BF)
@@ -193,22 +198,28 @@
             ka[pl.ds(xx * 4 + r, 18, stride=16), :] = kx[xx, pl.ds(r, 18, stride=4), :]
     kbuf[z] = ka[...].astype(BF)
 
-    def hop(way, step, part):
-        shard = (z + (nz - step if way == 0 else step)) % nz
-        piece = kbuf.at[shard, pl.ds(part * (288 // PARTS), 288 // PARTS)]
-        return remote(piece, piece, zs_sem.at[way, step, part], zr_sem.at[way, step, part], right if way == 0 else left)
-
-    hops = (nz // 2, nz - 1 - nz // 2)
-
-    def advance(step):
-        for part in range(PARTS):
-            for way in range(2):
-                if step < hops[way]:
-                    if step > 0:
-                        hop(way, step - 1, part).wait_recv()
-                    hop(way, step, part).start()
-
-    advance(0)
+    def hop(offset, step, part):
+        spot = (offset - step) % nz
+        piece = kbuf.at[(z + nz + offset) % nz, pl.ds(part * 144, 144)]
+        return remote(piece, piece, zs_sem.at[spot, part], zr_sem.at[spot, part], along_z(step))
+
+    def came(offset, part):
+        hop(offset, 0, part).wait_recv()
+
+    routes = {0: (3, -3, 1, -1), -3: (3, 1, -1), 3: (-3, 1, -1), -6: (1, -1), 6: (1, -1)}
+
+    def pass_on(first, second):
+        for part in range(2):
+            for offset in (first, second):
+                came(offset, part)
+                for step in routes[offset]:
+                    hop(offset, step, part).start()
+                if (offset, part) in ((-6, 0), (6, 1)):
+                    hop(offset, 2 if part == 0 else -2, part).start()
+
+    for part in range(2):
+        for step in routes[0]:
+            hop(0, step, part).start()
     for d in range(1, 4):
         xx = (x + d) % 4
         remote(ph.at[x], ph.at[x], ps_sem.at[xx], pr_sem.at[x], at(xx, me)).start()
@@ -263,29 +274,24 @@
 
     def wait_vectors(mm):
         remote(rows_of(mm), mrecv.at[mm], ms_sem.at[mm], mr_sem.at[mm], at(x, mm)).wait_recv()
-        remote(freq_ref, frecv.at[mm], fs_sem.at[mm], fr_sem.at[mm], at(x, mm)).wait_recv()
-
-    for step in range(8):
-        if step > 0:
-            advance(step)
-        else:
-            constant[0].wait()
-            constant[1].wait()
-            constant[2].wait()
-            own_modes.wait()
-        if step < 4:
-            xx = (x + step) % 4
-            if step > 0:
-                wait_window(xx)
-            weights(xx)
-        mm = (me + step) % 8
-        if step > 0:
-            wait_vectors(mm)
-        vectors(mm)
-    for way in range(2):
-        if hops[way]:
-            for part in range(PARTS):
-                hop(way, hops[way] - 1, part).wait_recv()
+        remote(fs, frecv.at[mm], fs_sem.at[mm], fr_sem.at[mm], at(x, mm)).wait_recv()
+
+    pass_on(-3, 3)
+    for copy in constant[:3]:
+        copy.wait()
+    own_modes.wait()
+    weights(x)
+    vectors(me)
+    pass_on(-6, 6)
+    for d in range(1, 4):
+        wait_window((x + d) % 4)
+        weights((x + d) % 4)
+    for d in range(1, 8):
+        wait_vectors((me + d) % 8)
+        vectors((me + d) % 8)
+    for offset in (-1, 1, -4, 4, -7, 7, -2, 2, -5, 5, 8):
+        for part in range(2):
+            came(offset, part)
 
     for d in range(1, 4):
         xx = (x + d) % 4
@@ -323,12 +329,18 @@
             bsend.at[xx * 8 + mm], brecv.at[sx, sm], bs_sem.at[xx * 8 + mm], br_sem.at[sx * 8 + sm], at(xx, mm)
         )
 
-    @pl.loop(1, 32)
+    @pl.loop(1, 4)
     def _(d):
-        xx, mm = (x + d // 8) % 4, (me + d) % 8
-        bsend[xx * 8 + mm] = band(xx, mm)
-        block(xx, mm, x, me).start()
-
+        xx = (x + d) % 4
+        for half in range(2):
+            for mm in range(half * 4, half * 4 + 4):
+                bsend[xx * 8 + mm] = band(xx, mm)
+            for mm in range(half * 4, half * 4 + 4):
+                block(xx, mm, x, me).start()
+
+    for d in range(1, 8):
+        bsend[x * 8 + (me + d) % 8] = band(x, (me + d) % 8)
+        block(x, (me + d) % 8, x, me).start()
     brecv[x, me] = band(x, me)
 
     @pl.loop(1, 32)
@@ -341,19 +353,25 @@
     for part in range(4):
         rhs[part * 640:(part + 1) * 640, :] = dot(blocks, order_ref[:, part * 256:(part + 1) * 256]).astype(BF)
 
-    def finish(mm):
-        done = dot(lhs[mm], rhs[...]) * scale[mm]
-        for ri in range(2):
-            of[pl.ds(ri, 144, stride=2), :] = done[:, ri * 128:(ri + 1) * 128]
-        return of[...].astype(BF)
-
-    @pl.loop(1, 8)
-    def _(d):
-        mm = (me + d) % 8
-        osend[mm] = finish(mm)
+    def finish(chip):
+        done = dot(lhs[pl.ds(chip * 2, 2)].reshape(288, 2560), rhs[...])
+        for n in range(2):
+            one = done[n * 144:(n + 1) * 144] * scale[chip * 2 + n]
+            for ri in range(2):
+                of[n, pl.ds(ri, 144, stride=2), :] = one[:, ri * 128:(ri + 1) * 128]
+            osend[chip * 2 + n] = of[n].astype(BF)
+
+    def send_out(mm):
         remote(osend.at[mm], o_ref.at[me], os_sem.at[mm], or_sem.at[me], at(x, mm)).start()
 
-    o_ref[me] = finish(me)
+    for d in (2, 1, 3):
+        chip = (me // 2 + d) % 4
+        finish(chip)
+        send_out(chip * 2 + me % 2)
+        send_out(chip * 2 + 1 - me % 2)
+    finish(me // 2)
+    send_out(me // 2 * 2 + 1 - me % 2)
+    o_ref[me] = osend[me]
 
     @pl.loop(1, 8)
     def _(d):
@@ -368,11 +386,13 @@
     for d in range(1, 8):
         mm = (me + d) % 8
         remote(rows_of(mm), mrecv.at[me], ms_sem.at[mm], mr_sem.at[me], at(x, mm)).wait_send()
-        remote(freq_ref, frecv.at[me], fs_sem.at[mm], fr_sem.at[me], at(x, mm)).wait_send()
-    for way in range(2):
-        for step in range(hops[way]):
-            for part in range(PARTS):
-                hop(way, step, part).wait_send()
+        remote(fs, frecv.at[me], fs_sem.at[mm], fr_sem.at[me], at(x, mm)).wait_send()
+    for part in range(2):
+        for offset, steps in routes.items():
+            for step in steps:
+                hop(offset, step, part).wait_send()
+    hop(-6, 2, 0).wait_send()
+    hop(6, -2, 1).wait_send()
 
     @pl.loop(1, 32)
     def _(d):
@@ -385,10 +405,9 @@
     small, large = constants(nz)
 
     g_rows = g_wann.reshape(4, 2, 18, 8, 128).transpose(0, 2, 3, 1, 4).reshape(1152, 128)
-    rot = jnp.pad(rot_k, ((0, 0), (0, 0), (0, 120)))
-    points = jnp.pad(qpoints.astype(BF), ((0, 125), (0, 64)))
+    rot = rot_k.transpose(0, 2, 1)
     rotq = rot_kq.transpose(1, 2, 3, 0).reshape(2048, 64)
-    freq = jnp.pad(frequencies.T, ((0, 6), (0, 64)), constant_values=1.0)
+    freq = frequencies.T
     modes = modes_vec.transpose(0, 2, 1, 3).reshape(1152, 288)
 
     vmem = pl.BlockSpec(memory_space=pltpu.VMEM)
@@ -409,6 +428,8 @@
             pltpu.VMEM((80, 2048), BF),
             pltpu.VMEM((2048, 512), BF),
             pltpu.VMEM((80, 512), F32),
+            pltpu.VMEM((8, 128), F32),
+            pltpu.VMEM((24, 128), F32),
             pltpu.VMEM((4, 80, 128), F32),
             pltpu.VMEM((4, 80, 128), BF),
             pltpu.VMEM((4, 80, 128), BF),
@@ -427,16 +448,16 @@
             pltpu.VMEM((8, 144, 2560), BF),
             pltpu.VMEM((8, 144, 1), F32),
             pltpu.VMEM((2560, 256), BF),
-            pltpu.VMEM((288, 128), F32),
+            pltpu.VMEM((2, 288, 128), F32),
             pltpu.VMEM((8, 288, 128), BF),
             sem((5,)),
             sem((4,)), sem((4,)), sem((4,)), sem((4,)), sem((4,)), sem((4,)), sem((8,)), sem((8,)), sem((8,)), sem((8,)),
-            sem((2, 8, PARTS)), sem((2, 8, PARTS)), sem((32,)), sem((32,)), sem((8,)), sem((8,)),
+            sem((16, 2)), sem((16, 2)), sem((32,)), sem((32,)), sem((8,)), sem((8,)),
         ],
         compiler_params=pltpu.CompilerParams(
             collective_id=0, has_side_effects=True, vmem_limit_bytes=56 * 1024 * 1024
         ),
-    )(win_start, win_count, g_rows, rot, points, rotq, freq, modes, *small, *large)
+    )(win_start, win_count, g_rows, rot, qpoints, rotq, freq, modes, *small, *large)
     return out.reshape(64, 18, 2, 128).transpose(0, 2, 1, 3)
 
 

time: 92.6 us -> 77.3 us (0.83)
  Pallas kernels: 82.1 us -> 70.9 us
  local copies, waits for them, and re-layouts: 9.56 us -> 6.25 us
    pallas_call x1, Pallas kernels: 82.1 us -> 70.9 us  [shards(): pl.pallas_call(functools.partial(kernel, nz), out_shape=jax.ShapeDtypeStr...]
    pad x3 -> x0, local copies, waits for them, and re-layouts: 2.53 us -> none  [the longest x1 1.31 us: shards(): freq = jnp.pad(frequencies.T, ((0, 6), (0, 64)), constant_values=1.0)]
    unnamed x2 -> x1, local copies, waits for them, and re-layouts: 3.06 us -> 2.28 us
where the time goes in v3:
time: 77.3 us; the launch traced here: 77.1 us
  Pallas kernels  70.9 us (92%)
  local copies, waits for them, and re-layouts  6.25 us (8%)
    pallas_call x1, Pallas kernels, shards(): pl.pallas_call(functools.partial(kernel, nz), out_shape=jax.ShapeDtypeStr...  70.9 us
    reshape x1, local copies, waits for them, and re-layouts, shards(): modes = modes_vec.transpose(0, 2, 1, 3).reshape(1152, 288)  3.97 us
    unnamed x1, local copies, waits for them, and re-layouts  2.28 us

profile of v3, /device:TPU:1, one launch (start us, length us, event | category | flops | bytes accessed | tf_op | source)
XLA Modules:
  0.0 77.1 jit_solution(13818099583868535153)
XLA Ops:
  0.0 4.0 %reshape.18.modes_ref = bf16[1152,288]{1,0:T(8,128)(2,1)} reshape(bf16[64,18,2,144]{3,2,1,0:T(2,128)(2,1)} %bitcast.15) | data formatting | bytes 1327104 | tf_op jit(solution)/shard_map/reshape | solution.py:411
  4.0 70.9 %shard_map.172 = bf16[8,288,128]{2,1,0:T(8,128)(2,1)} custom-call(s32[8]{0:T(128)} %ws_ref.1, s32[8]{0:T(128)} %wc_ref.1, bf16[1152,128]{1,0:T(8,128)(2,1)} %bitcast.17, bf16[2,8,32]{2,1,0:T(8,128)(2,1)} %bitcast.19, s32[3,64]{1,0:T(4,128)} %qp_ref.1, bf16[2048,64]{1,0:T(8,128)(2,1)} %bitcast.16, f32[18,64]{1,0:T(8,128)} %bitcast.18, ...), custom_call_target="tpu_custom_call" | custom-call | tf_op jit(solution)/shard_map/pallas_call | solution.py:417
  74.8 2.3 %copy.22 = bf16[64,2,18,128]{3,1,2,0:T(2,128)(2,1)} copy(bf16[64,2,18,128]{3,1,2,0:T(2,128)(2,1)} %bitcast.14) | data formatting | bytes 1179648

commit v4 on v3

--- a/solution.py
+++ b/solution.py
@@ -46,11 +46,10 @@
                     spread[par, q4, 0, m, q4, 1, b, par, 1, m, b] = 1
     spread = spread.reshape(2, 128, 2048)
 
-    pick = np.zeros((288, 1280), np.float32)
-    for ri in range(2):
-        for c in range(144):
-            for q4 in range(4):
-                pick[ri * 144 + c, ri * 640 + c // 18 * 80 + q4 * 20 + c % 18] = 1
+    pick = np.zeros((256, 640), np.float32)
+    for c in range(144):
+        for q4 in range(4):
+            pick[c, c // 18 * 80 + q4 * 20 + c % 18] = 1
     mask = np.zeros((2, 2, 4, 18, 8, 4, 20), np.float32)
     for par in range(2):
         for q4 in range(4):
@@ -80,18 +79,25 @@
     second = np.zeros((64, 64), np.float32)
     second[q, q // 2 % 8 * 8 + q % 2 * 4 + q // 16] = 1
 
+    gather = np.zeros((18, 4, 4, 4, 80), np.float32)
+    for c in range(18):
+        for xx in range(4):
+            for r4 in range(4):
+                gather[c, xx, r4, xx, c * 4 + r4] = 1
+    gather = gather.reshape(288, 320)
+
     modes = np.zeros((144, 24), np.float32)
     modes[np.arange(144), np.arange(144) % 18] = 1
     half = lambda a: jnp.asarray(a, BF)
-    small = [half(lattice), jnp.asarray(shift), half(bands), half(first), half(second), half(modes)]
+    small = [half(lattice), jnp.asarray(shift), half(bands), half(first), half(second), half(modes), half(gather)]
     return small, [half(spread), half(pick), half(mask), half(order)]
 
 
 def kernel(
     nz, ws_ref, wc_ref, g_ref, rot_ref, qp_ref, rotq_ref, freq_ref, modes_ref,
-    lattice_ref, shift_ref, bands_ref, first_ref, second_ref, rowmode_ref, spread_in, pick_in, mask_in, order_in, o_ref,
+    lattice_ref, shift_ref, bands_ref, first_ref, second_ref, rowmode_ref, gather_ref, spread_in, pick_in, mask_in, order_in, o_ref,
     spread_ref, pick_ref, mask_ref, order_ref,
-    gf, gl, kw, tf, qs, fs, kf, ksend, krecv, kx, ka, kbuf, ph, xf, win, wq, qbuf, bsend, brecv, mrecv, frecv, lhs, scale, rhs,
+    gf, gl, kw, tf, qs, fs, kf, ksend, kraw, kbuf, ph, xf, win, wq, qbuf, bsend, brecv, mrecv, mf, frecv, lhs, scale, rhs,
     of, osend, c_sem,
     ks_sem, kr_sem, ps_sem, pr_sem, ns_sem, nr_sem, ms_sem, mr_sem, fs_sem, fr_sem, zs_sem, zr_sem, bs_sem, br_sem,
     os_sem, or_sem,
@@ -110,8 +116,8 @@
             device_id=where, device_id_type=pl.DeviceIdType.MESH,
         )
 
-    def along_z(step):
-        return {"mode": me, "pb": x * nz + (z + nz + step) % nz}
+    def along_z(step, xx=None):
+        return {"mode": me, "pb": (x if xx is None else xx) * nz + (z + nz + step) % nz}
 
     barrier = pltpu.get_barrier_semaphore()
 
@@ -121,10 +127,15 @@
             barrier, inc=1, device_id=at((x + d // 8) % 4, (me + d) % 8), device_id_type=pl.DeviceIdType.MESH
         )
 
-    near = (-3, 3, -1, 1, -2, 2)
+    near = (3, -3, 1, -1)
     for step in near:
+        for xx in range(4):
+            pl.semaphore_signal(barrier, inc=1, device_id=along_z(step, xx), device_id_type=pl.DeviceIdType.MESH)
+    for step in (2, -2):
         pl.semaphore_signal(barrier, inc=1, device_id=along_z(step), device_id_type=pl.DeviceIdType.MESH)
 
+    qbuf[...] = jnp.zeros_like(qbuf)
+    mf[...] = jnp.zeros_like(mf)
     constant = [
         pltpu.make_async_copy(source, held, c_sem.at[n])
         for n, (source, held) in enumerate(
@@ -161,15 +172,24 @@
             kf[xx, pl.ds(r, 18, stride=4), :] = tf[r * 18:r * 18 + 18, xx * 128:(xx + 1) * 128]
     ksend[...] = kf[...].astype(BF)
 
-    pl.semaphore_wait(barrier, 31 + len(near))
-
-    for d in range(1, 4):
-        xx = (x + d) % 4
-        remote(ksend.at[xx], krecv.at[x], ks_sem.at[xx], kr_sem.at[x], at(xx, me)).start()
-    krecv[x] = ksend[x]
+    pl.semaphore_wait(barrier, 31 + 4 * len(near) + 2)
+
+    def first(slot, step, xx):
+        return remote(ksend.at[xx], kraw.at[z, x], ks_sem.at[slot, xx], kr_sem.at[slot, x], along_z(step, xx))
+
+    def first_came(slot, step, xx):
+        home = kraw.at[(z + nz - step) % nz, xx]
+        remote(ksend.at[xx], home, ks_sem.at[slot, xx], kr_sem.at[slot, xx], along_z(step, xx)).wait_recv()
+
+    for slot, step in enumerate(near):
+        for d in (2, 1, 3, 0):
+            first(slot, step, (x + d) % 4).start()
+    for d in range(1, 4):
+        first(4, 0, (x + d) % 4).start()
+    kraw[z, x] = ksend[x]
 
     def rows_of(mm):
-        return modes_ref.at[pl.ds(pl.multiple_of(mm * 144, 144), 144)]
+        return modes_ref.at[pl.ds(mm * 8, 8)]
 
     fs[...] = jnp.ones_like(fs)
     fs[0:18, 0:64] = freq_ref[...]
@@ -189,37 +209,34 @@
     ph[x, 0:64, :] = jnp.cos(angle).astype(BF)
     ph[x, 64:128, :] = jnp.sin(angle).astype(BF)
 
-    for d in range(1, 4):
-        xx = (x + d) % 4
-        remote(ksend.at[xx], krecv.at[xx], ks_sem.at[xx], kr_sem.at[xx], at(xx, me)).wait_recv()
-    kx[...] = krecv[...].astype(F32)
-    for xx in range(4):
-        for r in range(4):
-            ka[pl.ds(xx * 4 + r, 18, stride=16), :] = kx[xx, pl.ds(r, 18, stride=4), :]
-    kbuf[z] = ka[...].astype(BF)
-
     def hop(offset, step, part):
         spot = (offset - step) % nz
-        piece = kbuf.at[(z + nz + offset) % nz, pl.ds(part * 144, 144)]
+        piece = kraw.at[(z + nz + offset) % nz, pl.ds(part * 2, 2)]
         return remote(piece, piece, zs_sem.at[spot, part], zr_sem.at[spot, part], along_z(step))
 
     def came(offset, part):
-        hop(offset, 0, part).wait_recv()
-
-    routes = {0: (3, -3, 1, -1), -3: (3, 1, -1), 3: (-3, 1, -1), -6: (1, -1), 6: (1, -1)}
-
-    def pass_on(first, second):
+        if offset in (-3, 3):
+            slot = near.index(-offset)
+            for xx in (part * 2, part * 2 + 1):
+                first_came(slot, -offset, xx)
+        else:
+            hop(offset, 0, part).wait_recv()
+
+    routes = {-3: (3, 1, -1), 3: (-3, 1, -1), -6: (1, -1), 6: (1, -1)}
+
+    def pass_on(one, other):
         for part in range(2):
-            for offset in (first, second):
+            for offset in (one, other):
                 came(offset, part)
                 for step in routes[offset]:
                     hop(offset, step, part).start()
                 if (offset, part) in ((-6, 0), (6, 1)):
                     hop(offset, 2 if part == 0 else -2, part).start()
 
-    for part in range(2):
-        for step in routes[0]:
-            hop(0, step, part).start()
+    def assemble(offset):
+        shard = (z + nz + offset) % nz
+        kbuf[shard] = dot(gather_ref[...], kraw[shard].reshape(320, 128)).astype(BF)
+
     for d in range(1, 4):
         xx = (x + d) % 4
         remote(ph.at[x], ph.at[x], ps_sem.at[xx], pr_sem.at[x], at(xx, me)).start()
@@ -263,11 +280,15 @@
         low = (rest - middle.astype(F32)).astype(BF)
         by_row = dot(rowmode_ref[...], high) + dot(rowmode_ref[...], middle) + dot(rowmode_ref[...], low)
         scale[mm] = jnp.sum(jnp.where(diagonal, by_row, 0.0), axis=1, keepdims=True)
-        both = dot(mrecv[mm], pick_ref[...]).astype(BF)
-        for par in range(2):
-            for ri in range(2):
+        rows = mrecv[mm].reshape(288, 144)
+        mf[0] = rows[:, :128].astype(F32)
+        mf[1, :, 0:16] = rows[:, 128:].astype(F32)
+        for ri in range(2):
+            halves = [mf[n, pl.ds(ri, 144, stride=2), :].astype(BF) for n in range(2)]
+            spreaded = dot(jnp.concatenate(halves, axis=1), pick_ref[...]).astype(BF)
+            for par in range(2):
                 start = (par * 2 + ri) * 640
-                lhs[mm, :, start:start + 640] = both[:, ri * 640:(ri + 1) * 640] * mask_ref[par]
+                lhs[mm, :, start:start + 640] = spreaded * mask_ref[par]
 
     def wait_window(xx):
         remote(win.at[xx], win.at[xx], ns_sem.at[xx], nr_sem.at[xx], at(xx, me)).wait_recv()
@@ -283,24 +304,32 @@
     weights(x)
     vectors(me)
     pass_on(-6, 6)
+    for offset in (-3, 3, -6, 6):
+        assemble(offset)
     for d in range(1, 4):
         wait_window((x + d) % 4)
         weights((x + d) % 4)
+    for d in range(1, 4):
+        first_came(4, 0, (x + d) % 4)
+    assemble(0)
+    for slot, step in ((2, 1), (3, -1)):
+        for xx in range(4):
+            first_came(slot, step, xx)
+        assemble(-step)
     for d in range(1, 8):
         wait_vectors((me + d) % 8)
         vectors((me + d) % 8)
-    for offset in (-1, 1, -4, 4, -7, 7, -2, 2, -5, 5, 8):
+    for offset in (-2, 2, -4, 4, -5, 5, -7, 7, 8):
         for part in range(2):
             came(offset, part)
+        assemble(offset)
 
     for d in range(1, 4):
         xx = (x + d) % 4
         remote(ph.at[xx], ph.at[xx], ps_sem.at[xx], pr_sem.at[xx], at(xx, me)).wait_recv()
-    qbuf[...] = jnp.zeros_like(qbuf)
     turn = lax.broadcasted_iota(jnp.int32, (64, 128), 1) < 64
 
-    @pl.loop(0, 9)
-    def _(cp):
+    def sum_pair(cp):
         pair = [
             kbuf[:, pl.ds(pl.multiple_of((cp * 2 + p) * 16, 16), 16), :].reshape(nr, 128) for p in range(2)
         ]
@@ -313,6 +342,11 @@
                 for par in range(2):
                     qbuf[par, pl.ds(xx * 640 + cp * 2 + p, 32, stride=20), :] = total[par * 32:(par + 1) * 32]
 
+    @pl.loop(0, 3)
+    def _(third):
+        for u in range(3):
+            sum_pair(third * 3 + u)
+
     row = lax.broadcasted_iota(jnp.int32, (80, 256), 0)
 
     def band(xx, mm):
@@ -329,9 +363,9 @@
             bsend.at[xx * 8 + mm], brecv.at[sx, sm], bs_sem.at[xx * 8 + mm], br_sem.at[sx * 8 + sm], at(xx, mm)
         )
 
-    @pl.loop(1, 4)
-    def _(d):
-        xx = (x + d) % 4
+    @pl.loop(0, 3)
+    def _(n):
+        xx = (x + 2 - n + n // 2 * 3) % 4
         for half in range(2):
             for mm in range(half * 4, half * 4 + 4):
                 bsend[xx * 8 + mm] = band(xx, mm)
@@ -343,15 +377,20 @@
         block(x, (me + d) % 8, x, me).start()
     brecv[x, me] = band(x, me)
 
-    @pl.loop(1, 32)
-    def _(d):
-        xx, mm = (x + d // 8) % 4, (me + d) % 8
-        block(xx, mm, xx, mm).wait_recv()
-
     constant[3].wait()
-    blocks = jnp.concatenate([brecv[xx].reshape(640, 128) for xx in range(4)], axis=1)
-    for part in range(4):
-        rhs[part * 640:(part + 1) * 640, :] = dot(blocks, order_ref[:, part * 256:(part + 1) * 256]).astype(BF)
+    for d in (0, 1, 3, 2):
+        xx = (x + d) % 4
+
+        @pl.loop(1 if d == 0 else 0, 8)
+        def _(n):
+            block(xx, (me + n) % 8, xx, (me + n) % 8).wait_recv()
+
+        placed = dot(brecv[xx].reshape(640, 128), order_ref[pl.ds(pl.multiple_of(xx * 128, 128), 128), :]).astype(BF)
+        for part in range(4):
+            here = placed[:, part * 256:(part + 1) * 256]
+            if d > 0:
+                here = here + rhs[part * 640:(part + 1) * 640, :]
+            rhs[part * 640:(part + 1) * 640, :] = here
 
     def finish(chip):
         done = dot(lhs[pl.ds(chip * 2, 2)].reshape(288, 2560), rhs[...])
@@ -378,9 +417,12 @@
         mm = (me + d) % 8
         remote(osend.at[mm], o_ref.at[mm], os_sem.at[mm], or_sem.at[mm], at(x, mm)).wait()
 
+    for slot, step in enumerate(near):
+        for xx in range(4):
+            first(slot, step, xx).wait_send()
     for d in range(1, 4):
         xx = (x + d) % 4
-        remote(ksend.at[xx], krecv.at[x], ks_sem.at[xx], kr_sem.at[x], at(xx, me)).wait_send()
+        first(4, 0, xx).wait_send()
         remote(ph.at[x], ph.at[x], ps_sem.at[xx], pr_sem.at[x], at(xx, me)).wait_send()
         remote(win.at[x], win.at[x], ns_sem.at[xx], nr_sem.at[x], at(xx, me)).wait_send()
     for d in range(1, 8):
@@ -408,7 +450,7 @@
     rot = rot_k.transpose(0, 2, 1)
     rotq = rot_kq.transpose(1, 2, 3, 0).reshape(2048, 64)
     freq = frequencies.T
-    modes = modes_vec.transpose(0, 2, 1, 3).reshape(1152, 288)
+    modes = modes_vec.transpose(0, 2, 1, 3)
 
     vmem = pl.BlockSpec(memory_space=pltpu.VMEM)
     smem = pl.BlockSpec(memory_space=pltpu.SMEM)
@@ -417,11 +459,11 @@
     out = pl.pallas_call(
         functools.partial(kernel, nz),
         out_shape=jax.ShapeDtypeStruct((8, 288, 128), BF),
-        in_specs=[smem, smem] + [vmem] * 12 + [whole] * 4,
+        in_specs=[smem, smem] + [vmem] * 5 + [whole] + [vmem] * 7 + [whole] * 4,
         out_specs=vmem,
         scratch_shapes=[
             pltpu.VMEM((2, 128, 2048), BF),
-            pltpu.VMEM((288, 1280), BF),
+            pltpu.VMEM((256, 640), BF),
             pltpu.VMEM((2, 144, 640), BF),
             pltpu.VMEM((512, 1024), BF),
             pltpu.VMEM((1152, 128), F32),
@@ -432,9 +474,7 @@
             pltpu.VMEM((24, 128), F32),
             pltpu.VMEM((4, 80, 128), F32),
             pltpu.VMEM((4, 80, 128), BF),
-            pltpu.VMEM((4, 80, 128), BF),
-            pltpu.VMEM((4, 80, 128), F32),
-            pltpu.VMEM((288, 128), F32),
+            pltpu.VMEM((nz, 4, 80, 128), BF),
             pltpu.VMEM((nz, 288, 128), BF),
             pltpu.VMEM((4, 128, nz * 16), BF),
             pltpu.VMEM((4, 512, 64), F32),
@@ -443,7 +483,8 @@
             pltpu.VMEM((2, 2560, 128), F32),
             pltpu.VMEM((32, 80, 128), BF),
             pltpu.VMEM((4, 8, 80, 128), BF),
-            pltpu.VMEM((8, 144, 288), BF),
+            pltpu.VMEM((8, 8, 18, 2, 144), BF),
+            pltpu.VMEM((2, 288, 128), F32),
             pltpu.VMEM((8, 24, 128), F32),
             pltpu.VMEM((8, 144, 2560), BF),
             pltpu.VMEM((8, 144, 1), F32),
@@ -451,7 +492,7 @@
             pltpu.VMEM((2, 288, 128), F32),
             pltpu.VMEM((8, 288, 128), BF),
             sem((5,)),
-            sem((4,)), sem((4,)), sem((4,)), sem((4,)), sem((4,)), sem((4,)), sem((8,)), sem((8,)), sem((8,)), sem((8,)),
+            sem((5, 4)), sem((5, 4)), sem((4,)), sem((4,)), sem((4,)), sem((4,)), sem((8,)), sem((8,)), sem((8,)), sem((8,)),
             sem((16, 2)), sem((16, 2)), sem((32,)), sem((32,)), sem((8,)), sem((8,)),
         ],
         compiler_params=pltpu.CompilerParams(

time: 77.3 us -> 73.3 us (0.948)
  local copies, waits for them, and re-layouts: 6.25 us -> 2.28 us
    reshape x1 -> x0, local copies, waits for them, and re-layouts: 3.97 us -> none  [shards(): modes = modes_vec.transpose(0, 2, 1, 3).reshape(1152, 288)]
where the time goes in v4:
time: 73.3 us; the launch traced here: 73.1 us
  Pallas kernels  70.9 us (97%)
  local copies, waits for them, and re-layouts  2.28 us (3%)
    pallas_call x1, Pallas kernels, shards(): pl.pallas_call(functools.partial(kernel, nz), out_shape=jax.ShapeDtypeStr...  70.9 us
    unnamed x1, local copies, waits for them, and re-layouts  2.28 us

profile of v4, /device:TPU:1, one launch (start us, length us, event | category | flops | bytes accessed | tf_op | source)
XLA Modules:
  0.0 73.1 jit_solution(14676440688951849058)
XLA Ops:
  0.0 70.9 %shard_map.181 = bf16[8,288,128]{2,1,0:T(8,128)(2,1)} custom-call(s32[8]{0:T(128)} %ws_ref.1, s32[8]{0:T(128)} %wc_ref.1, bf16[1152,128]{1,0:T(8,128)(2,1)} %bitcast.17, bf16[2,8,32]{2,1,0:T(8,128)(2,1)} %bitcast.19, s32[3,64]{1,0:T(4,128)} %qp_ref.1, bf16[2048,64]{1,0:T(8,128)(2,1)} %bitcast.16, f32[18,64]{1,0:T(8,128)} %bitcast.18, ...), custom_call_target="tpu_custom_call" | custom-call | tf_op jit(solution)/shard_map/pallas_call | solution.py:459
  70.9 2.3 %copy.22 = bf16[64,2,18,128]{3,1,2,0:T(2,128)(2,1)} copy(bf16[64,2,18,128]{3,1,2,0:T(2,128)(2,1)} %bitcast.14) | data formatting | bytes 1179648

commit v5 on v4

--- a/solution.py
+++ b/solution.py
@@ -175,18 +175,17 @@
     pl.semaphore_wait(barrier, 31 + 4 * len(near) + 2)
 
     def first(slot, step, xx):
-        return remote(ksend.at[xx], kraw.at[z, x], ks_sem.at[slot, xx], kr_sem.at[slot, x], along_z(step, xx))
+        return remote(ksend.at[xx], kraw.at[slot, x], ks_sem.at[slot, xx], kr_sem.at[slot, x], along_z(step, xx))
 
     def first_came(slot, step, xx):
-        home = kraw.at[(z + nz - step) % nz, xx]
-        remote(ksend.at[xx], home, ks_sem.at[slot, xx], kr_sem.at[slot, xx], along_z(step, xx)).wait_recv()
+        remote(ksend.at[xx], kraw.at[slot, xx], ks_sem.at[slot, xx], kr_sem.at[slot, xx], along_z(step, xx)).wait_recv()
 
     for slot, step in enumerate(near):
         for d in (2, 1, 3, 0):
             first(slot, step, (x + d) % 4).start()
     for d in range(1, 4):
         first(4, 0, (x + d) % 4).start()
-    kraw[z, x] = ksend[x]
+    kraw[4, x] = ksend[x]
 
     def rows_of(mm):
         return modes_ref.at[pl.ds(mm * 8, 8)]
@@ -211,42 +210,39 @@
 
     def hop(offset, step, part):
         spot = (offset - step) % nz
-        piece = kraw.at[(z + nz + offset) % nz, pl.ds(part * 2, 2)]
+        piece = kbuf.at[(z + nz + offset) % nz, pl.ds(part * 144, 144)]
         return remote(piece, piece, zs_sem.at[spot, part], zr_sem.at[spot, part], along_z(step))
 
     def came(offset, part):
-        if offset in (-3, 3):
-            slot = near.index(-offset)
-            for xx in (part * 2, part * 2 + 1):
-                first_came(slot, -offset, xx)
-        else:
-            hop(offset, 0, part).wait_recv()
+        hop(offset, 0, part).wait_recv()
+
+    def assemble(slot, step):
+        for xx in range(4):
+            first_came(slot, step, xx)
+        kbuf[(z + nz - step) % nz] = dot(gather_ref[...], kraw[slot].reshape(320, 128)).astype(BF)
 
     routes = {-3: (3, 1, -1), 3: (-3, 1, -1), -6: (1, -1), 6: (1, -1)}
-
-    def pass_on(one, other):
-        for part in range(2):
-            for offset in (one, other):
-                came(offset, part)
-                for step in routes[offset]:
-                    hop(offset, step, part).start()
-                if (offset, part) in ((-6, 0), (6, 1)):
-                    hop(offset, 2 if part == 0 else -2, part).start()
-
-    def assemble(offset):
-        shard = (z + nz + offset) % nz
-        kbuf[shard] = dot(gather_ref[...], kraw[shard].reshape(320, 128)).astype(BF)
 
     for d in range(1, 4):
         xx = (x + d) % 4
         remote(ph.at[x], ph.at[x], ps_sem.at[xx], pr_sem.at[x], at(xx, me)).start()
 
-    @pl.loop(0, 32)
+    @pl.loop(0, 32, unroll=4)
     def _(i):
         both = [rotq_ref[pl.ds(pl.multiple_of(ri * 1024 + i * 32, 32), 32), :] for ri in range(2)]
         flipped = dot_t(second_ref[...], jnp.concatenate(both, axis=0))
         for q4 in range(4):
             xf[q4, pl.ds(i, 16, stride=32), :] = flipped[q4 * 16:(q4 + 1) * 16]
+
+    assemble(0, 3)
+    assemble(1, -3)
+    for part in range(2):
+        hop(-3, 3, part).start()
+        hop(3, -3, part).start()
+    for part in range(2):
+        for offset in (-3, 3):
+            for step in (1, -1):
+                hop(offset, step, part).start()
 
     lane_m = lax.broadcasted_iota(jnp.int32, (256, 128), 1) % 16
     for t in range(8):
@@ -297,55 +293,48 @@
         remote(rows_of(mm), mrecv.at[mm], ms_sem.at[mm], mr_sem.at[mm], at(x, mm)).wait_recv()
         remote(fs, frecv.at[mm], fs_sem.at[mm], fr_sem.at[mm], at(x, mm)).wait_recv()
 
-    pass_on(-3, 3)
     for copy in constant[:3]:
         copy.wait()
     own_modes.wait()
     weights(x)
+    for part in range(2):
+        for offset in (-6, 6):
+            came(offset, part)
+            for step in (1, -1):
+                hop(offset, step, part).start()
+            if (offset, part) in ((-6, 0), (6, 1)):
+                hop(offset, 2 if part == 0 else -2, part).start()
     vectors(me)
-    pass_on(-6, 6)
-    for offset in (-3, 3, -6, 6):
-        assemble(offset)
     for d in range(1, 4):
         wait_window((x + d) % 4)
         weights((x + d) % 4)
-    for d in range(1, 4):
-        first_came(4, 0, (x + d) % 4)
-    assemble(0)
-    for slot, step in ((2, 1), (3, -1)):
-        for xx in range(4):
-            first_came(slot, step, xx)
-        assemble(-step)
     for d in range(1, 8):
         wait_vectors((me + d) % 8)
         vectors((me + d) % 8)
+    for d in range(1, 4):
+        first_came(4, 0, (x + d) % 4)
+    kbuf[z] = dot(gather_ref[...], kraw[4].reshape(320, 128)).astype(BF)
+    assemble(2, 1)
+    assemble(3, -1)
     for offset in (-2, 2, -4, 4, -5, 5, -7, 7, 8):
         for part in range(2):
             came(offset, part)
-        assemble(offset)
 
     for d in range(1, 4):
         xx = (x + d) % 4
         remote(ph.at[xx], ph.at[xx], ps_sem.at[xx], pr_sem.at[xx], at(xx, me)).wait_recv()
     turn = lax.broadcasted_iota(jnp.int32, (64, 128), 1) < 64
 
-    def sum_pair(cp):
-        pair = [
-            kbuf[:, pl.ds(pl.multiple_of((cp * 2 + p) * 16, 16), 16), :].reshape(nr, 128) for p in range(2)
-        ]
-        both = dot(ph[...].reshape(512, nr), jnp.concatenate(pair, axis=1))
-        for p in range(2):
-            for xx in range(4):
-                along = both[xx * 128:xx * 128 + 64, p * 128:(p + 1) * 128]
-                across = pltpu.roll(both[xx * 128 + 64:xx * 128 + 128, p * 128:(p + 1) * 128], 64, 1)
+    def sums(xx):
+        for cp in range(9):
+            pair = [kbuf[:, (cp * 2 + p) * 16:(cp * 2 + p) * 16 + 16, :].reshape(nr, 128) for p in range(2)]
+            both = dot(ph[xx], jnp.concatenate(pair, axis=1))
+            for p in range(2):
+                along = both[0:64, p * 128:(p + 1) * 128]
+                across = pltpu.roll(both[64:128, p * 128:(p + 1) * 128], 64, 1)
                 total = along + jnp.where(turn, -across, across)
                 for par in range(2):
                     qbuf[par, pl.ds(xx * 640 + cp * 2 + p, 32, stride=20), :] = total[par * 32:(par + 1) * 32]
-
-    @pl.loop(0, 3)
-    def _(third):
-        for u in range(3):
-            sum_pair(third * 3 + u)
 
     row = lax.broadcasted_iota(jnp.int32, (80, 256), 0)
 
@@ -366,12 +355,14 @@
     @pl.loop(0, 3)
     def _(n):
         xx = (x + 2 - n + n // 2 * 3) % 4
+        sums(xx)
         for half in range(2):
             for mm in range(half * 4, half * 4 + 4):
                 bsend[xx * 8 + mm] = band(xx, mm)
             for mm in range(half * 4, half * 4 + 4):
                 block(xx, mm, x, me).start()
 
+    sums(x)
     for d in range(1, 8):
         bsend[x * 8 + (me + d) % 8] = band(x, (me + d) % 8)
         block(x, (me + d) % 8, x, me).start()
@@ -474,7 +465,7 @@
             pltpu.VMEM((24, 128), F32),
             pltpu.VMEM((4, 80, 128), F32),
             pltpu.VMEM((4, 80, 128), BF),
-            pltpu.VMEM((nz, 4, 80, 128), BF),
+            pltpu.VMEM((5, 4, 80, 128), BF),
             pltpu.VMEM((nz, 288, 128), BF),
             pltpu.VMEM((4, 128, nz * 16), BF),
             pltpu.VMEM((4, 512, 64), F32),

time: 73.3 us -> 70 us (0.955)
  Pallas kernels: 70.9 us -> 67.6 us
    pallas_call x1, Pallas kernels: 70.9 us -> 67.6 us  [shards(): pl.pallas_call(functools.partial(kernel, nz), out_shape=jax.ShapeDtypeStr...]
where the time goes in v5:
time: 70 us; the launch traced here: 69.9 us
  Pallas kernels  67.6 us (97%)
  local copies, waits for them, and re-layouts  2.28 us (3%)
    pallas_call x1, Pallas kernels, shards(): pl.pallas_call(functools.partial(kernel, nz), out_shape=jax.ShapeDtypeStr...  67.6 us
    unnamed x1, local copies, waits for them, and re-layouts  2.28 us

profile of v5, /device:TPU:1, one launch (start us, length us, event | category | flops | bytes accessed | tf_op | source)
XLA Modules:
  0.0 69.9 jit_solution(17080150523465020886)
XLA Ops:
  0.0 67.6 %shard_map.181 = bf16[8,288,128]{2,1,0:T(8,128)(2,1)} custom-call(s32[8]{0:T(128)} %ws_ref.1, s32[8]{0:T(128)} %wc_ref.1, bf16[1152,128]{1,0:T(8,128)(2,1)} %bitcast.17, bf16[2,8,32]{2,1,0:T(8,128)(2,1)} %bitcast.19, s32[3,64]{1,0:T(4,128)} %qp_ref.1, bf16[2048,64]{1,0:T(8,128)(2,1)} %bitcast.16, f32[18,64]{1,0:T(8,128)} %bitcast.18, ...), custom_call_target="tpu_custom_call" | custom-call | tf_op jit(solution)/shard_map/pallas_call | solution.py:450
  67.6 2.3 %copy.22 = bf16[64,2,18,128]{3,1,2,0:T(2,128)(2,1)} copy(bf16[64,2,18,128]{3,1,2,0:T(2,128)(2,1)} %bitcast.14) | data formatting | bytes 1179648

commit v6 on v5

--- a/solution.py
+++ b/solution.py
@@ -50,11 +50,10 @@
     for c in range(144):
         for q4 in range(4):
             pick[c, c // 18 * 80 + q4 * 20 + c % 18] = 1
-    mask = np.zeros((2, 2, 4, 18, 8, 4, 20), np.float32)
-    for par in range(2):
-        for q4 in range(4):
-            mask[par, par, q4, :, :, q4, :] = 1
-    mask = mask.reshape(2, 144, 640)
+    mask = np.zeros((4, 18, 8, 4, 20), np.float32)
+    for q4 in range(4):
+        mask[q4, :, :, q4, :] = 1
+    mask = mask.reshape(72, 640)
 
     order = np.zeros((4, 2, 2, 16, 2, 2, 2, 2, 16, 8), np.float32)
     for xx in range(4):
@@ -90,15 +89,18 @@
     modes[np.arange(144), np.arange(144) % 18] = 1
     half = lambda a: jnp.asarray(a, BF)
     small = [half(lattice), jnp.asarray(shift), half(bands), half(first), half(second), half(modes), half(gather)]
-    return small, [half(spread), half(pick), half(mask), half(order)]
+    return small, [half(spread), half(pick), jnp.asarray(mask), half(order)]
 
 
 def kernel(
-    nz, ws_ref, wc_ref, g_ref, rot_ref, qp_ref, rotq_ref, freq_ref, modes_ref,
-    lattice_ref, shift_ref, bands_ref, first_ref, second_ref, rowmode_ref, gather_ref, spread_in, pick_in, mask_in, order_in, o_ref,
+    nz, ws_in, wc_in, g_in, rot_in, qp_in, rotq_in, freq_in, modes_ref,
+    lattice_in, shift_in, bands_in, first_in, second_in, rowmode_in, gather_in, spread_in, pick_in, mask_in, order_in,
+    o_ref,
+    ws_ref, wc_ref, g_ref, rot_ref, qp_ref, rotq_ref, freq_ref,
+    lattice_ref, shift_ref, bands_ref, first_ref, second_ref, rowmode_ref, gather_ref,
     spread_ref, pick_ref, mask_ref, order_ref,
     gf, gl, kw, tf, qs, fs, kf, ksend, kraw, kbuf, ph, xf, win, wq, qbuf, bsend, brecv, mrecv, mf, frecv, lhs, scale, rhs,
-    of, osend, c_sem,
+    of, osend, c_sem, i_sem,
     ks_sem, kr_sem, ps_sem, pr_sem, ns_sem, nr_sem, ms_sem, mr_sem, fs_sem, fr_sem, zs_sem, zr_sem, bs_sem, br_sem,
     os_sem, or_sem,
 ):
@@ -134,6 +136,19 @@
     for step in (2, -2):
         pl.semaphore_signal(barrier, inc=1, device_id=along_z(step), device_id_type=pl.DeviceIdType.MESH)
 
+    fetched = [
+        pltpu.make_async_copy(source, held, i_sem.at[n])
+        for n, (source, held) in enumerate(
+            (
+                (g_in, g_ref), (rot_in, rot_ref), (bands_in, bands_ref), (ws_in, ws_ref), (wc_in, wc_ref),
+                (qp_in, qp_ref), (rotq_in, rotq_ref), (freq_in, freq_ref), (lattice_in, lattice_ref),
+                (shift_in, shift_ref), (first_in, first_ref), (second_in, second_ref), (rowmode_in, rowmode_ref),
+                (gather_in, gather_ref),
+            )
+        )
+    ]
+    for copy in fetched:
+        copy.start()
     qbuf[...] = jnp.zeros_like(qbuf)
     mf[...] = jnp.zeros_like(mf)
     constant = [
@@ -145,6 +160,8 @@
     for copy in constant:
         copy.start()
 
+    for copy in fetched[:3]:
+        copy.wait()
     lane = lax.broadcasted_iota(jnp.int32, (32, 512), 1)
     lane_i = lane % 32
     turn_b = lambda ri: lax.dot_general(
@@ -173,6 +190,9 @@
     ksend[...] = kf[...].astype(BF)
 
     pl.semaphore_wait(barrier, 31 + 4 * len(near) + 2)
+
+    for copy in fetched[3:]:
+        copy.wait()
 
     def first(slot, step, xx):
         return remote(ksend.at[xx], kraw.at[slot, x], ks_sem.at[slot, xx], kr_sem.at[slot, x], along_z(step, xx))
@@ -281,10 +301,10 @@
         mf[1, :, 0:16] = rows[:, 128:].astype(F32)
         for ri in range(2):
             halves = [mf[n, pl.ds(ri, 144, stride=2), :].astype(BF) for n in range(2)]
-            spreaded = dot(jnp.concatenate(halves, axis=1), pick_ref[...]).astype(BF)
+            spreaded = dot(jnp.concatenate(halves, axis=1), pick_ref[...])
             for par in range(2):
-                start = (par * 2 + ri) * 640
-                lhs[mm, :, start:start + 640] = spreaded * mask_ref[par]
+                own_rows = spreaded[par * 72:(par + 1) * 72] * mask_ref[...]
+                lhs[par, mm, 0:72, ri * 640:(ri + 1) * 640] = own_rows.astype(BF)
 
     def wait_window(xx):
         remote(win.at[xx], win.at[xx], ns_sem.at[xx], nr_sem.at[xx], at(xx, me)).wait_recv()
@@ -384,11 +404,13 @@
             rhs[part * 640:(part + 1) * 640, :] = here
 
     def finish(chip):
-        done = dot(lhs[pl.ds(chip * 2, 2)].reshape(288, 2560), rhs[...])
+        for par in range(2):
+            done = dot(lhs[par, pl.ds(chip * 2, 2)].reshape(160, 1280), rhs[par * 1280:(par + 1) * 1280, :])
+            for n in range(2):
+                one = done[n * 80:n * 80 + 72] * scale[chip * 2 + n, par * 72:(par + 1) * 72]
+                for ri in range(2):
+                    of[n, pl.ds(par * 144 + ri, 72, stride=2), :] = one[:, ri * 128:(ri + 1) * 128]
         for n in range(2):
-            one = done[n * 144:(n + 1) * 144] * scale[chip * 2 + n]
-            for ri in range(2):
-                of[n, pl.ds(ri, 144, stride=2), :] = one[:, ri * 128:(ri + 1) * 128]
             osend[chip * 2 + n] = of[n].astype(BF)
 
     def send_out(mm):
@@ -444,18 +466,19 @@
     modes = modes_vec.transpose(0, 2, 1, 3)
 
     vmem = pl.BlockSpec(memory_space=pltpu.VMEM)
-    smem = pl.BlockSpec(memory_space=pltpu.SMEM)
     whole = pl.BlockSpec(memory_space=pl.ANY)
     sem = pltpu.SemaphoreType.DMA
     out = pl.pallas_call(
         functools.partial(kernel, nz),
         out_shape=jax.ShapeDtypeStruct((8, 288, 128), BF),
-        in_specs=[smem, smem] + [vmem] * 5 + [whole] + [vmem] * 7 + [whole] * 4,
+        in_specs=[whole] * 19,
         out_specs=vmem,
         scratch_shapes=[
+            pltpu.SMEM((8,), jnp.int32), pltpu.SMEM((8,), jnp.int32),
+            *[pltpu.VMEM(a.shape, a.dtype) for a in (g_rows, rot, qpoints, rotq, freq, *small)],
             pltpu.VMEM((2, 128, 2048), BF),
             pltpu.VMEM((256, 640), BF),
-            pltpu.VMEM((2, 144, 640), BF),
+            pltpu.VMEM((72, 640), F32),
             pltpu.VMEM((512, 1024), BF),
             pltpu.VMEM((1152, 128), F32),
             pltpu.VMEM((80, 2048), BF),
@@ -477,12 +500,12 @@
             pltpu.VMEM((8, 8, 18, 2, 144), BF),
             pltpu.VMEM((2, 288, 128), F32),
             pltpu.VMEM((8, 24, 128), F32),
-            pltpu.VMEM((8, 144, 2560), BF),
+            pltpu.VMEM((2, 8, 80, 1280), BF),
             pltpu.VMEM((8, 144, 1), F32),
             pltpu.VMEM((2560, 256), BF),
             pltpu.VMEM((2, 288, 128), F32),
             pltpu.VMEM((8, 288, 128), BF),
-            sem((5,)),
+            sem((5,)), sem((14,)),
             sem((5, 4)), sem((5, 4)), sem((4,)), sem((4,)), sem((4,)), sem((4,)), sem((8,)), sem((8,)), sem((8,)), sem((8,)),
             sem((16, 2)), sem((16, 2)), sem((32,)), sem((32,)), sem((8,)), sem((8,)),
         ],

time: 70 us -> 67.9 us (0.970)
  Pallas kernels: 67.6 us -> 65.4 us
    pallas_call x1, Pallas kernels: 67.6 us -> 65.4 us  [shards(): pl.pallas_call(functools.partial(kernel, nz), out_shape=jax.ShapeDtypeStr...]
where the time goes in v6:
time: 67.9 us; the launch traced here: 67.7 us
  Pallas kernels  65.4 us (96%)
  local copies, waits for them, and re-layouts  2.28 us (3%)
    pallas_call x1, Pallas kernels, shards(): pl.pallas_call(functools.partial(kernel, nz), out_shape=jax.ShapeDtypeStr...  65.4 us
    unnamed x1, local copies, waits for them, and re-layouts  2.28 us

profile of v6, /device:TPU:1, one launch (start us, length us, event | category | flops | bytes accessed | tf_op | source)
XLA Modules:
  0.0 67.7 jit_solution(12488368230387148003)
XLA Ops:
  0.0 65.4 %shard_map.181 = bf16[8,288,128]{2,1,0:T(8,128)(2,1)} custom-call(s32[8]{0:T(128)} %ws_in.1, s32[8]{0:T(128)} %wc_in.1, bf16[1152,128]{1,0:T(8,128)(2,1)} %bitcast.17, bf16[2,8,32]{2,1,0:T(8,128)(2,1)} %bitcast.19, s32[3,64]{1,0:T(4,128)} %qp_in.1, bf16[2048,64]{1,0:T(8,128)(2,1)} %bitcast.16, f32[18,64]{1,0:T(8,128)} %bitcast.18, ...), custom_call_target="tpu_custom_call" | custom-call | tf_op jit(solution)/shard_map/pallas_call | solution.py:471
  65.5 2.3 %copy.22 = bf16[64,2,18,128]{3,1,2,0:T(2,128)(2,1)} copy(bf16[64,2,18,128]{3,1,2,0:T(2,128)(2,1)} %bitcast.14) | data formatting | bytes 1179648

commit v7 on v6

--- a/solution.py
+++ b/solution.py
@@ -140,7 +140,7 @@
         pltpu.make_async_copy(source, held, i_sem.at[n])
         for n, (source, held) in enumerate(
             (
-                (g_in, g_ref), (rot_in, rot_ref), (bands_in, bands_ref), (ws_in, ws_ref), (wc_in, wc_ref),
+                (rot_in, rot_ref), (bands_in, bands_ref), (g_in, g_ref), (ws_in, ws_ref), (wc_in, wc_ref),
                 (qp_in, qp_ref), (rotq_in, rotq_ref), (freq_in, freq_ref), (lattice_in, lattice_ref),
                 (shift_in, shift_ref), (first_in, first_ref), (second_in, second_ref), (rowmode_in, rowmode_ref),
                 (gather_in, gather_ref),
@@ -149,18 +149,13 @@
     ]
     for copy in fetched:
         copy.start()
-    qbuf[...] = jnp.zeros_like(qbuf)
-    mf[...] = jnp.zeros_like(mf)
     constant = [
         pltpu.make_async_copy(source, held, c_sem.at[n])
         for n, (source, held) in enumerate(
             ((spread_in, spread_ref), (pick_in, pick_ref), (mask_in, mask_ref), (order_in, order_ref))
         )
     ]
-    for copy in constant:
-        copy.start()
-
-    for copy in fetched[:3]:
+    for copy in fetched[:2]:
         copy.wait()
     lane = lax.broadcasted_iota(jnp.int32, (32, 512), 1)
     lane_i = lane % 32
@@ -173,10 +168,11 @@
     for ri in range(2):
         part = parts[ri]
 
-        @pl.loop(0, 32)
+        @pl.loop(0, 32, unroll=4)
         def _(i):
             kw[pl.ds(pl.multiple_of(ri * 1024 + i * 32, 32), 32), :] = jnp.where(lane_i == i, part, 0.0).astype(BF)
 
+    fetched[2].wait()
     gf[...] = g_ref[...].astype(F32)
     for ri in range(2):
         for k in range(8):
@@ -191,9 +187,6 @@
 
     pl.semaphore_wait(barrier, 31 + 4 * len(near) + 2)
 
-    for copy in fetched[3:]:
-        copy.wait()
-
     def first(slot, step, xx):
         return remote(ksend.at[xx], kraw.at[slot, x], ks_sem.at[slot, xx], kr_sem.at[slot, x], along_z(step, xx))
 
@@ -206,6 +199,12 @@
     for d in range(1, 4):
         first(4, 0, (x + d) % 4).start()
     kraw[4, x] = ksend[x]
+    for copy in constant:
+        copy.start()
+    for copy in fetched[3:]:
+        copy.wait()
+    qbuf[...] = jnp.zeros_like(qbuf)
+    mf[...] = jnp.zeros_like(mf)
 
     def rows_of(mm):
         return modes_ref.at[pl.ds(mm * 8, 8)]
@@ -254,11 +253,10 @@
         for q4 in range(4):
             xf[q4, pl.ds(i, 16, stride=32), :] = flipped[q4 * 16:(q4 + 1) * 16]
 
-    assemble(0, 3)
-    assemble(1, -3)
-    for part in range(2):
-        hop(-3, 3, part).start()
-        hop(3, -3, part).start()
+    for slot, step in ((0, 3), (1, -3)):
+        assemble(slot, step)
+        for part in range(2):
+            hop(-step, step, part).start()
     for part in range(2):
         for offset in (-3, 3):
             for step in (1, -1):
@@ -324,6 +322,11 @@
                 hop(offset, step, part).start()
             if (offset, part) in ((-6, 0), (6, 1)):
                 hop(offset, 2 if part == 0 else -2, part).start()
+    for d in range(1, 4):
+        first_came(4, 0, (x + d) % 4)
+    kbuf[z] = dot(gather_ref[...], kraw[4].reshape(320, 128)).astype(BF)
+    assemble(2, 1)
+    assemble(3, -1)
     vectors(me)
     for d in range(1, 4):
         wait_window((x + d) % 4)
@@ -331,11 +334,6 @@
     for d in range(1, 8):
         wait_vectors((me + d) % 8)
         vectors((me + d) % 8)
-    for d in range(1, 4):
-        first_came(4, 0, (x + d) % 4)
-    kbuf[z] = dot(gather_ref[...], kraw[4].reshape(320, 128)).astype(BF)
-    assemble(2, 1)
-    assemble(3, -1)
     for offset in (-2, 2, -4, 4, -5, 5, -7, 7, 8):
         for part in range(2):
             came(offset, part)
@@ -376,10 +374,10 @@
     def _(n):
         xx = (x + 2 - n + n // 2 * 3) % 4
         sums(xx)
-        for half in range(2):
-            for mm in range(half * 4, half * 4 + 4):
+        for half in range(4):
+            for mm in range(half * 2, half * 2 + 2):
                 bsend[xx * 8 + mm] = band(xx, mm)
-            for mm in range(half * 4, half * 4 + 4):
+            for mm in range(half * 2, half * 2 + 2):
                 block(xx, mm, x, me).start()
 
     sums(x)

time: 67.9 us -> 67.1 us (0.988)
  Pallas kernels: 65.4 us -> 64.7 us
    pallas_call x1, Pallas kernels: 65.4 us -> 64.7 us  [shards(): pl.pallas_call(functools.partial(kernel, nz), out_shape=jax.ShapeDtypeStr...]
where the time goes in v7:
time: 67.1 us; the launch traced here: 67 us
  Pallas kernels  64.7 us (96%)
  local copies, waits for them, and re-layouts  2.28 us (3%)
    pallas_call x1, Pallas kernels, shards(): pl.pallas_call(functools.partial(kernel, nz), out_shape=jax.ShapeDtypeStr...  64.7 us
    unnamed x1, local copies, waits for them, and re-layouts  2.28 us

profile of v7, /device:TPU:1, one launch (start us, length us, event | category | flops | bytes accessed | tf_op | source)
XLA Modules:
  0.0 67.0 jit_solution(9390795061715442049)
XLA Ops:
  0.0 64.7 %shard_map.181 = bf16[8,288,128]{2,1,0:T(8,128)(2,1)} custom-call(s32[8]{0:T(128)} %ws_in.1, s32[8]{0:T(128)} %wc_in.1, bf16[1152,128]{1,0:T(8,128)(2,1)} %bitcast.17, bf16[2,8,32]{2,1,0:T(8,128)(2,1)} %bitcast.19, s32[3,64]{1,0:T(4,128)} %qp_in.1, bf16[2048,64]{1,0:T(8,128)(2,1)} %bitcast.16, f32[18,64]{1,0:T(8,128)} %bitcast.18, ...), custom_call_target="tpu_custom_call" | custom-call | tf_op jit(solution)/shard_map/pallas_call | solution.py:469
  64.7 2.3 %copy.22 = bf16[64,2,18,128]{3,1,2,0:T(2,128)(2,1)} copy(bf16[64,2,18,128]{3,1,2,0:T(2,128)(2,1)} %bitcast.14) | data formatting | bytes 1179648
